TPU v7x, 256 devices: a whole 4x4x8 slice. The times are simulated.
256 devices in a mesh: vid: 64 (over y, z_hi, x), aud: 4 (over z_lo, core).
Axes of the slice: x: 4, y: 4, z: 8 (z_hi: 4, z_lo: 2; z = z_hi * 2 + z_lo), core: 2. Of those that a mesh axis runs over, the one named last changes fastest.
Arguments:
- video_query: bfloat16 [16384, 3072], P(('vid', 'aud')), may hold values from -66 to 66
- video_key: bfloat16 [16384, 3072], P(('vid', 'aud')), may hold values from -4 to 4
- video_value: bfloat16 [16384, 3072], P(('vid', 'aud')), may hold values from -6 to 6
- video_cotan: bfloat16 [16384, 3072], P(('vid', 'aud')), may hold values from -6 to 6
- audio_query: bfloat16 [1024, 3072], P('vid', 'aud'), may hold values from -66 to 66
- audio_key: bfloat16 [1024, 3072], P('vid', 'aud'), may hold values from -4 to 4
- audio_value: bfloat16 [1024, 3072], P('vid', 'aud'), may hold values from -6 to 6
- audio_cotan: bfloat16 [1024, 3072], P('vid', 'aud'), may hold values from -6 to 6
- alignment: int32 [1024], replicated, may hold values from 0 to 15, as said below
Outputs:
- video_cross_output: bfloat16 [16384, 3072], P(('vid', 'aud'))
- audio_cross_output: bfloat16 [1024, 3072], P('vid', 'aud')
- video_query_grad: bfloat16 [16384, 3072], P(('vid', 'aud'))
- video_key_grad: bfloat16 [16384, 3072], P(('vid', 'aud'))
- video_value_grad: bfloat16 [16384, 3072], P(('vid', 'aud'))
- audio_query_grad: bfloat16 [1024, 3072], P('vid', 'aud')
- audio_key_grad: bfloat16 [1024, 3072], P('vid', 'aud')
- audio_value_grad: bfloat16 [1024, 3072], P('vid', 'aud')
Inputs may be any that keep to these rules, and one draw needn't show every extreme that they name: `alignment`: non-decreasing along the audio tokens; the first is 0 and the last 15.
All inputs are finite; a program needn't handle non-finite values.
Results may differ from a plain program's by a relative error of at most 0.035.
Values may be sent and summed in bfloat16 or wider, within the bound.
No kernel may reach another device: no remote copies, remote signals or barrier semaphores. Data moves between devices by JAX's collectives and lax.ppermute only.
A program may use at most 128 MiB of HBM per device.

v0:
```python
import jax
import jax.numpy as jnp
from jax import lax
from jax.sharding import PartitionSpec as P

DH = 128
FRAMES = 16


BIAS_SLOPE = 0.25


def split_into_heads(array, head_count):
    return array.reshape(array.shape[0], head_count, DH)


def merge_heads(array):
    return array.reshape(array.shape[0], array.shape[1] * array.shape[2])


def per_device(
    video_query,
    video_key,
    video_value,
    video_cotan,
    audio_query,
    audio_key,
    audio_value,
    audio_cotan,
    alignment,
):
    score_scale = DH ** (-0.5)
    video_query_rows, video_key_rows, video_value_rows, video_output_cotangent = (
        lax.all_to_all(video_query, "aud", split_axis=1, concat_axis=0, tiled=True),
        lax.all_to_all(video_key, "aud", split_axis=1, concat_axis=0, tiled=True),
        lax.all_to_all(video_value, "aud", split_axis=1, concat_axis=0, tiled=True),
        lax.all_to_all(video_cotan, "aud", split_axis=1, concat_axis=0, tiled=True),
    )
    audio_query_rows, audio_key_rows, audio_value_rows, audio_output_cotangent = (
        lax.all_gather(audio_query, "vid", axis=0, tiled=True),
        lax.all_gather(audio_key, "vid", axis=0, tiled=True),
        lax.all_gather(audio_value, "vid", axis=0, tiled=True),
        lax.all_gather(audio_cotan, "vid", axis=0, tiled=True),
    )
    local_rows = video_query_rows.shape[0]
    head_count = video_query_rows.shape[1] // DH
    owned = audio_query.shape[0]
    frame_tok = local_rows * lax.axis_size("vid") // FRAMES
    positions = lax.axis_index("vid") * local_rows + jnp.arange(local_rows, dtype=jnp.int32)
    frames = positions // frame_tok
    score_bias = -BIAS_SLOPE * jnp.abs(frames[:, None] - alignment[None, :]).astype(jnp.float32)
    vquery_h = split_into_heads(video_query_rows, head_count)
    video_key_heads = split_into_heads(video_key_rows, head_count)
    vvalue_h = split_into_heads(video_value_rows, head_count)
    vcotan_h = split_into_heads(video_output_cotangent, head_count)
    audio_query_heads = split_into_heads(audio_query_rows, head_count)
    akey_h = split_into_heads(audio_key_rows, head_count)
    avalue_h = split_into_heads(audio_value_rows, head_count)
    acotan_h = split_into_heads(audio_output_cotangent, head_count)
    scores = (
        jnp.einsum("qhd,khd->hqk", vquery_h, akey_h, preferred_element_type=jnp.float32)
        * score_scale
        + score_bias[None]
    )
    peaks = jnp.max(scores, axis=2, keepdims=True)
    raised = jnp.exp(scores - peaks)
    totals = jnp.sum(raised, axis=2, keepdims=True)
    video_attn = jnp.einsum(
        "hqk,khd->qhd", raised.astype(jnp.bfloat16), avalue_h, preferred_element_type=jnp.float32
    ) / jnp.transpose(totals, (1, 0, 2))
    probs = raised / totals
    probs_low = probs.astype(jnp.bfloat16)
    inner = jnp.transpose(jnp.sum(vcotan_h.astype(jnp.float32) * video_attn, axis=2), (1, 0))[
        :, :, None
    ]
    dprobs = jnp.einsum("qhd,khd->hqk", vcotan_h, avalue_h, preferred_element_type=jnp.float32)
    dscores = (probs * (dprobs - inner)).astype(jnp.bfloat16)
    video_query_gradient = (
        jnp.einsum("hqk,khd->qhd", dscores, akey_h, preferred_element_type=jnp.float32)
        * score_scale
    )
    cross = (
        jnp.einsum(
            "unf,jnf->nuj", audio_query_heads, video_key_heads, preferred_element_type=jnp.float32
        )
        * score_scale
        + score_bias.T[None]
    )
    audio_peaks = lax.pmax(jnp.max(cross, axis=2), "vid")
    audio_raised = jnp.exp(cross - audio_peaks[:, :, None])
    partial_totals = jnp.sum(audio_raised, axis=2)
    partial_out = jnp.einsum(
        "kbj,jky->bky",
        audio_raised.astype(jnp.bfloat16),
        vvalue_h,
        preferred_element_type=jnp.float32,
    )
    full_out, audio_totals = lax.psum((partial_out, partial_totals), "vid")
    full_attn = full_out / jnp.transpose(audio_totals, (1, 0))[:, :, None]
    audio_inner = jnp.transpose(jnp.sum(acotan_h.astype(jnp.float32) * full_attn, axis=2), (1, 0))
    audio_attn = lax.dynamic_slice_in_dim(full_attn, lax.axis_index("vid") * owned, owned, 0)
    audio_probs = audio_raised / audio_totals[:, :, None]
    audio_dprobs = jnp.einsum(
        "unf,jnf->nuj", acotan_h, vvalue_h, preferred_element_type=jnp.float32
    )
    audio_score_gradient = (audio_probs * (audio_dprobs - audio_inner[:, :, None])).astype(
        jnp.bfloat16
    )
    video_key_gradient = (
        jnp.einsum(
            "har,ahd->rhd",
            audio_score_gradient,
            audio_query_heads,
            preferred_element_type=jnp.float32,
        )
        * score_scale
    )
    video_value_gradient = jnp.einsum(
        "har,ahd->rhd",
        audio_probs.astype(jnp.bfloat16),
        acotan_h,
        preferred_element_type=jnp.float32,
    )
    akey_part = merge_heads(
        jnp.einsum("hqk,qhd->khd", dscores, vquery_h, preferred_element_type=jnp.float32)
        * score_scale
    )
    avalue_part = merge_heads(
        jnp.einsum("hqk,qhd->khd", probs_low, vcotan_h, preferred_element_type=jnp.float32)
    )
    aquery_part = merge_heads(
        jnp.einsum(
            "kbj,jky->bky",
            audio_score_gradient,
            video_key_heads,
            preferred_element_type=jnp.float32,
        )
        * score_scale
    )
    audio_query_gradient, audio_key_gradient, audio_value_gradient = (
        lax.psum_scatter(aquery_part, "vid", scatter_dimension=0, tiled=True),
        lax.psum_scatter(akey_part, "vid", scatter_dimension=0, tiled=True),
        lax.psum_scatter(avalue_part, "vid", scatter_dimension=0, tiled=True),
    )
    video_parts = (
        merge_heads(video_attn).astype(jnp.bfloat16),
        merge_heads(video_query_gradient).astype(jnp.bfloat16),
        merge_heads(video_key_gradient).astype(jnp.bfloat16),
        merge_heads(video_value_gradient).astype(jnp.bfloat16),
    )
    video_cross_output, video_query_grad, video_key_grad, video_value_grad = (
        lax.all_to_all(video_parts[0], "aud", split_axis=0, concat_axis=1, tiled=True),
        lax.all_to_all(video_parts[1], "aud", split_axis=0, concat_axis=1, tiled=True),
        lax.all_to_all(video_parts[2], "aud", split_axis=0, concat_axis=1, tiled=True),
        lax.all_to_all(video_parts[3], "aud", split_axis=0, concat_axis=1, tiled=True),
    )
    audio_cross_output = merge_heads(audio_attn).astype(jnp.bfloat16)
    return (
        video_cross_output,
        audio_cross_output,
        video_query_grad,
        video_key_grad,
        video_value_grad,
        audio_query_gradient.astype(jnp.bfloat16),
        audio_key_gradient.astype(jnp.bfloat16),
        audio_value_gradient.astype(jnp.bfloat16),
    )


def solution(mesh):
    placed = (
        P(("vid", "aud"), None),
        P(("vid", "aud"), None),
        P(("vid", "aud"), None),
        P(("vid", "aud"), None),
        P("vid", "aud"),
        P("vid", "aud"),
        P("vid", "aud"),
        P("vid", "aud"),
        P(),
    )
    return jax.shard_map(
        per_device,
        mesh=mesh,
        in_specs=placed,
        out_specs=(
            P(("vid", "aud"), None),
            P("vid", "aud"),
            P(("vid", "aud"), None),
            P(("vid", "aud"), None),
            P(("vid", "aud"), None),
            P("vid", "aud"),
            P("vid", "aud"),
            P("vid", "aud"),
        ),
        check_vma=False,
    )
```

profile of v0, /device:TPU:33, one launch (start us, length us, event | category | flops | bytes accessed | tf_op | source)
XLA Modules:
  0.0 1983.2 jit_solution(16931431801431776360)
XLA Ops:
  10.0 1.8 copy.176
  11.7 5.6 all-to-all-start.2
  17.3 1.8 copy.175
  19.1 3.8 all-to-all-done.2
  22.9 5.3 all-to-all-start.3
  28.2 1.8 copy.177
  31.7 2.3 all-to-all-done.3
  34.0 5.9 all-to-all-start
  40.3 47.7 %all-gather.9.cloned.1.call-done = bf16[1024,768]{1,0:T(8,128)(2,1)} async-done(((bf16[16,768]{1,0:T(8,128)(2,1)}), bf16[1024,768]{1,0:T(8,128)(2,1)}) %all-gather.9.cloned.1.call-update) | async-done | bytes 1572880 | tf_op jit(solution)/shard_map/all_gather | solution.py:40
  88.1 1.7 copy.113
  89.8 4.3 fusion.1
  94.1 323.2 %pmax.7 = f32[6,1024]{1,0:T(8,128)} all-reduce(f32[6,1024]{1,0:T(8,128)} %get-tuple-element.15), channel_id=1, replica_groups=mesh['vid'=64,'aud'=4] {'vid'}, use_global_device_ids=true, to_apply=%region_3.4 | all-reduce | flops 6144 | bytes 49152 | tf_op jit(solution)/shard_map/pmax | solution.py:89
  417.3 6.2 fusion.22
  423.6 1.8 copy.174
  425.4 62.1 %all-to-all-start.4 = ((bf16[64,4,768]{2,0,1:T(8,128)(2,1)}), bf16[64,4,768]{2,0,1:T(8,128)(2,1)}, u32[]{:S(2)}, u32[]{:S(2)}) async-start(bf16[64,4,768]{2,0,1:T(8,128)(2,1)} %bitcast.84), calls=%async_computation.4 | async-start | bytes 786432 | tf_op jit(solution)/shard_map/all_to_all | solution.py:37
  487.7 1.7 reshape.175
  489.8 3.3 all-to-all-done.4
  495.6 2.6 copy.107
  498.1 2.6 fusion
  500.8 1.5 fusion.3
  502.3 3.3 fusion.12
  505.6 3.5 copy.145
  509.4 2.8 copy.110
  512.2 6.1 multiply_reduce_fusion.1
  518.3 2.7 multiply_convert_fusion.1
  521.0 2.7 convolution_multiply_fusion
  523.7 3.6 copy.143
  527.4 1.7 copy.128
  529.2 1.7 copy.131
  530.8 4.8 fusion.6
  535.6 321.3 %psum.15 = f32[6,1024]{1,0:T(8,128)} all-reduce(f32[6,1024]{1,0:T(8,128)} %fusion.6), channel_id=1, replica_groups=mesh['vid'=64,'aud'=4] {'vid'}, use_global_device_ids=true, to_apply=%region_6.7 | all-reduce | flops 6144 | bytes 49152 | tf_op jit(solution)/shard_map/psum | solution.py:98
  856.9 312.8 %all-reduce.2.cloned.1.call-done = f32[1024,6,128]{2,0,1:T(8,128)} async-done(((f32[1024,6,128]{2,0,1:T(8,128)}), f32[1024,6,128]{2,0,1:T(8,128)}) %all-reduce.2.cloned.1.call-update) | async-done | bytes 3145744 | tf_op jit(solution)/shard_map/psum | solution.py:98
  1169.6 4.8 multiply_reduce_fusion
  1174.5 4.1 multiply_convert_fusion
  1178.6 2.6 convolution_multiply_fusion.1
  1181.2 3.7 copy.141
  1186.5 48.5 %all-to-all-start.1 = ((bf16[4,64,768]{2,1,0:T(8,128)(2,1)}), bf16[4,64,768]{2,1,0:T(8,128)(2,1)S(1)}, u32[]{:S(2)}, u32[]{:S(2)}) async-start(bf16[4,64,768]{2,1,0:T(8,128)(2,1)} %convert_element_type.93), calls=%async_computation.1 | async-start | bytes 786432 | tf_op jit(solution)/shard_map/all_to_all | solution.py:152
  1235.0 2.9 fusion.37
  1240.9 5.4 all-to-all-start.5
  1246.2 4.9 fusion.33
  1252.7 4.9 all-to-all-start.7
  1257.5 2.9 fusion.36
  1261.9 1.7 all-to-all-done.7
  1263.6 5.2 all-to-all-start.6
  1272.5 2.4 all-to-all-done.6
  1275.7 190.4 %reduce-scatter.8.cloned.1.call-done = f32[16,768]{1,0:T(8,128)} async-done(((f32[1024,768]{1,0:T(8,128)}), f32[16,768]{1,0:T(8,128)}) %reduce-scatter.8.cloned.1.call-update) | async-done | bytes 49168 | tf_op jit(solution)/shard_map/reduce_scatter | solution.py:143
  1467.5 253.0 %reduce-scatter.6.cloned.1.call-done = f32[16,768]{1,0:T(8,128)} async-done(((f32[1024,768]{1,0:T(8,128)}), f32[16,768]{1,0:T(8,128)}) %reduce-scatter.6.cloned.1.call-update) | async-done | bytes 49168 | tf_op jit(solution)/shard_map/reduce_scatter | solution.py:142
  1722.0 253.0 %reduce-scatter.4.cloned.1.call-done = f32[16,768]{1,0:T(8,128)} async-done(((f32[1024,768]{1,0:T(8,128)}), f32[16,768]{1,0:T(8,128)}) %reduce-scatter.4.cloned.1.call-update) | async-done | bytes 49168 | tf_op jit(solution)/shard_map/reduce_scatter | solution.py:141
  (96 shorter events, 24.6 us)
Async XLA Ops:
  7.2 80.9 %all-gather.9.cloned.1.call-start = ((), (), s32[]{:S(2)}) async-start(), calls=%async_computation.13 | async-start | bytes 1597440 | tf_op jit(solution)/shard_map/all_gather | solution.py:40
  7.9 487.7 %all-gather.5.cloned.1.call-start = ((), (), s32[]{:S(2)}) async-start(), calls=%async_computation.11 | async-start | bytes 1597440 | tf_op jit(solution)/shard_map/all_gather | solution.py:41
  8.7 500.8 %all-gather.7.cloned.1.call-start = ((), (), s32[]{:S(2)}) async-start(), calls=%async_computation.12 | async-start | bytes 1597440 | tf_op jit(solution)/shard_map/all_gather | solution.py:42
  9.4 518.0 %all-gather.11.cloned.1.call-start = ((), (), s32[]{:S(2)}) async-start(), calls=%async_computation.15 | async-start | bytes 1597440 | tf_op jit(solution)/shard_map/all_gather | solution.py:43
  11.7 11.1 all-to-all-start.2
  22.9 11.1 all-to-all-start.3
  34.0 391.4 %all-to-all-start = ((bf16[64,4,768]{2,0,1:T(8,128)(2,1)}), bf16[64,4,768]{2,0,1:T(8,128)(2,1)}, u32[]{:S(2)}, u32[]{:S(2)}) async-start(bf16[64,4,768]{2,0,1:T(8,128)(2,1)} %bitcast.87), calls=%async_computation | async-start | bytes 786432 | tf_op jit(solution)/shard_map/all_to_all | solution.py:34
  39.9 1129.8 %all-reduce.2.cloned.1.call-start = ((), (), s32[]{:S(2)}) async-start(), calls=%async_computation.14 | async-start | bytes 6291456 | tf_op jit(solution)/shard_map/psum | solution.py:98
  40.3 383.2 %copy-start.11 = (bf16[256,6,128]{2,1,0:T(8,128)(2,1)}, bf16[256,6,128]{2,1,0:T(8,128)(2,1)S(1)}, u32[]{:S(2)}) copy-start(bf16[256,6,128]{2,1,0:T(8,128)(2,1)S(1)} %reshape.180) | copy-start | bytes 1179652
  89.8 333.8 %copy-start.3 = (bf16[1024,768]{0,1:T(8,128)(2,1)}, bf16[1024,768]{0,1:T(8,128)(2,1)S(1)}, u32[]{:S(2)}) copy-start(bf16[1024,768]{0,1:T(8,128)(2,1)S(1)} %copy.113) | copy-start | bytes 4718596
  417.3 70.1 %copy-start.21 = (s32[1024]{0:T(1024)S(1)}, s32[1024]{0:T(1024)}, u32[]{:S(2)}) copy-start(s32[1024]{0:T(1024)} %param.17) | copy-start | bytes 12292
  425.4 67.7 %all-to-all-start.4 = ((bf16[64,4,768]{2,0,1:T(8,128)(2,1)}), bf16[64,4,768]{2,0,1:T(8,128)(2,1)}, u32[]{:S(2)}, u32[]{:S(2)}) async-start(bf16[64,4,768]{2,0,1:T(8,128)(2,1)} %bitcast.84), calls=%async_computation.4 | async-start | bytes 786432 | tf_op jit(solution)/shard_map/all_to_all | solution.py:37
  487.4 978.7 %reduce-scatter.8.cloned.1.call-start = ((), (), s32[]{:S(2)}) async-start(), calls=%async_computation.18 | async-start | bytes 3194880 | tf_op jit(solution)/shard_map/reduce_scatter | solution.py:143
  487.7 14.6 copy-start.1
  489.8 11.0 copy-start.7
  498.1 4.2 copy-start.15
  500.8 4.8 copy-start
  509.2 1211.4 %reduce-scatter.6.cloned.1.call-start = ((), (), s32[]{:S(2)}) async-start(), calls=%async_computation.17 | async-start | bytes 3194880 | tf_op jit(solution)/shard_map/reduce_scatter | solution.py:142
  509.4 8.9 slice-start
  512.2 6.1 slice-start.1
  512.2 6.1 copy-start.2
  512.2 6.1 copy-start.13
  512.2 6.1 copy-start.16
  518.3 2.7 copy-start.8
  521.0 2.7 copy-start.9
  527.3 1447.6 %reduce-scatter.4.cloned.1.call-start = ((), (), s32[]{:S(2)}) async-start(), calls=%async_computation.16 | async-start | bytes 3194880 | tf_op jit(solution)/shard_map/reduce_scatter | solution.py:141
  529.1 645.3 %copy-start.5 = (bf16[1024,768]{0,1:T(8,128)(2,1)}, bf16[1024,768]{0,1:T(8,128)(2,1)S(1)}, u32[]{:S(2)}) copy-start(bf16[1024,768]{0,1:T(8,128)(2,1)S(1)} %copy.128) | copy-start | bytes 4718596
  530.8 643.6 %copy-start.12 = (bf16[256,6,128]{2,1,0:T(8,128)(2,1)S(1)}, bf16[256,6,128]{2,1,0:T(8,128)(2,1)}, u32[]{:S(2)}) copy-start(bf16[256,6,128]{2,1,0:T(8,128)(2,1)} %copy-done.11) | copy-start | bytes 1179652
  1169.6 4.8 copy-start.17
  1169.6 4.8 copy-start.19
  1178.6 2.6 copy-start.10
  1181.2 3.7 copy-start.14
  1181.2 53.8 %copy-start.6 = (bf16[1024,768]{0,1:T(8,128)(2,1)S(1)}, bf16[1024,768]{0,1:T(8,128)(2,1)}, u32[]{:S(2)}) copy-start(bf16[1024,768]{0,1:T(8,128)(2,1)} %copy.107) | copy-start | bytes 4718596
  1185.3 61.0 %copy-start.18 = (f32[6,1024]{1,0:T(8,128)S(1)}, f32[6,1024]{1,0:T(8,128)}, u32[]{:S(2)}) copy-start(f32[6,1024]{1,0:T(8,128)} %pmax.7) | copy-start | bytes 73732
  1185.3 61.0 %copy-start.20 = (f32[6,1024]{1,0:T(8,128)S(1)}, f32[6,1024]{1,0:T(8,128)}, u32[]{:S(2)}) copy-start(f32[6,1024]{1,0:T(8,128)} %psum.15) | copy-start | bytes 73732
  1186.5 54.4 %all-to-all-start.1 = ((bf16[4,64,768]{2,1,0:T(8,128)(2,1)}), bf16[4,64,768]{2,1,0:T(8,128)(2,1)S(1)}, u32[]{:S(2)}, u32[]{:S(2)}) async-start(bf16[4,64,768]{2,1,0:T(8,128)(2,1)} %convert_element_type.93), calls=%async_computation.1 | async-start | bytes 786432 | tf_op jit(solution)/shard_map/all_to_all | solution.py:152
  1240.9 11.8 all-to-all-start.5
  1246.2 11.3 copy-start.4
  1252.7 11.0 all-to-all-start.7
  1263.6 11.3 all-to-all-start.6
Sparse Core Ops, SparseCore 0:
  11.3 76.7 all-gather.8
  91.4 74.2 all-gather.4
  168.9 74.3 all-gather.6
  246.5 74.0 all-gather.10
  423.7 745.8 all-reduce.1
  1175.0 291.0 reduce-scatter.7
  1471.7 248.8 reduce-scatter.5
  1726.1 248.8 reduce-scatter.3
where the time goes:
time: 1990 us; the launch traced here: 1980 us
  waiting for transfers between devices  1070 us (54%)
  blocking collectives  645 us (32%)
  starting transfers between devices  143 us (7%)
  matrix products  45.2 us (2%)
  local copies, waits for them, and re-layouts  44.6 us (2%)
    pmax x1, blocking collectives, per_device(): audio_peaks = lax.pmax(jnp.max(cross, axis=2), 'vid')  323 us
    psum x1, blocking collectives, per_device(): full_out, audio_totals = lax.psum((partial_out, partial_totals), 'vid')  321 us
    psum x1, waiting for transfers between devices, per_device(): full_out, audio_totals = lax.psum((partial_out, partial_totals), 'vid')  313 us
    reduce_scatter x1, waiting for transfers between devices, per_device(): lax.psum_scatter(akey_part, 'vid', scatter_dimension=0, tiled=True)  253 us
    reduce_scatter x1, waiting for transfers between devices, per_device(): lax.psum_scatter(aquery_part, 'vid', scatter_dimension=0, tiled=True)  253 us
    reduce_scatter x1, waiting for transfers between devices, per_device(): lax.psum_scatter(avalue_part, 'vid', scatter_dimension=0, tiled=True)  190 us
    all_to_all x1, starting transfers between devices, per_device(): lax.all_to_all(video_cotan, 'aud', split_axis=1, concat_axis=0, tiled=True)  62.1 us
    all_to_all x1, starting transfers between devices, per_device(): lax.all_to_all(video_parts[0], 'aud', split_axis=0, concat_axis=1, tiled=...  48.5 us
  transfers between devices with their start and end apart: 16, of which 11 were waited for; matrix products, arithmetic and copies ran while one was open for 5% of the time, Pallas kernels for 0%

commit v1 on v0

v1 whole, which is shorter than its diff:
```python
import math

import jax
import jax.numpy as jnp
from jax import lax
from jax.experimental import pallas as pl
from jax.experimental.pallas import tpu as pltpu
from jax.sharding import Mesh
from jax.sharding import PartitionSpec as P

DH = 128
FRAMES = 16
BIAS_SLOPE = 0.25
SCALE = DH ** (-0.5)
LOG2E = math.log2(math.e)

AXES = (("y", 4), ("zh", 4), ("xh", 2), ("xl", 2), ("zl", 2), ("core", 2))
NAMES = tuple(name for name, _ in AXES)
VID = ("y", "zh", "xh", "xl")
AUD = ("zl", "core")
HEADS8 = ("zl", "core", "xl")
PLANE = ("zh", "xh", "xl")
VMEM = 56 * 1024 * 1024
LONG = pl.CostEstimate(flops=5 * 10 ** 10, bytes_accessed=0, transcendentals=0)


def mm(a, b, contract):
    return lax.dot_general(
        a, b, ((contract[0], contract[1]), ((), ())), preferred_element_type=jnp.float32
    )


def rows_of(ref, array):
    return ref[:, array].reshape(ref.shape[0] * ref.shape[2], DH)


def audio_stats_kernel(start, qg0, qg1, qg2, qg3, kv, out):
    rows = kv.shape[0] * kv.shape[2]
    keys, values = rows_of(kv, 0), rows_of(kv, 1)
    for block, ref in enumerate((qg0, qg1, qg2, qg3)):
        width = ref.shape[0] * ref.shape[2]
        lanes = pl.ds(pl.multiple_of(start[block], width), width)
        scores = mm(keys, rows_of(ref, 0), ((1,), (1,)))
        peak = jnp.max(scores, axis=0, keepdims=True)
        raised = jnp.exp2((scores - peak) * (SCALE * LOG2E))
        total = jnp.sum(raised, axis=0, keepdims=True)
        dprobs = mm(values, rows_of(ref, 1), ((1,), (1,)))
        inner = jnp.sum(raised * dprobs, axis=0, keepdims=True)
        out[0, 0:1, lanes] = peak * SCALE + jnp.log(total)
        out[0, 1:2, lanes] = inner / total


def audio_grad_kernel(
    start, qg0, qg1, qg2, qg3, kv, stats, od0, od1, od2, od3, *refs
):
    kvgrad, probs_all, ds_all = refs[:8], refs[8], refs[9]
    keys = jnp.concatenate([kv[start[4 + m], 0] for m in range(8)], axis=0)
    values = jnp.concatenate([kv[start[4 + m], 1] for m in range(8)], axis=0)
    queries, cotans = [], []
    for block, (ref, dst) in enumerate(zip((qg0, qg1, qg2, qg3), (od0, od1, od2, od3))):
        width = ref.shape[0] * ref.shape[2]
        lanes = pl.ds(pl.multiple_of(start[block], width), width)
        query = rows_of(ref, 0)
        cotan = rows_of(ref, 1)
        queries.append(query)
        cotans.append(cotan)
        scores = mm(keys, query, ((1,), (1,)))
        probs = jnp.exp2(scores * (SCALE * LOG2E) - stats[0, 0:1, lanes] * LOG2E)
        dprobs = mm(values, cotan, ((1,), (1,)))
        dscores = (probs * (dprobs - stats[0, 1:2, lanes])).astype(jnp.bfloat16)
        probs = probs.astype(jnp.bfloat16)
        here = slice(block * width, (block + 1) * width)
        probs_all[:, here] = probs
        ds_all[:, here] = dscores
        out = jnp.transpose(mm(values, probs, ((0,), (0,)))).astype(jnp.bfloat16)
        qgrad = jnp.transpose(mm(keys, dscores, ((0,), (0,))) * SCALE).astype(jnp.bfloat16)
        shape = (ref.shape[0], ref.shape[2], DH)
        dst[:, 0] = out.reshape(shape)
        dst[:, 1] = qgrad.reshape(shape)
    kgrad = mm(ds_all[...], jnp.concatenate(queries, axis=0), ((1,), (0,))) * SCALE
    vgrad = mm(probs_all[...], jnp.concatenate(cotans, axis=0), ((1,), (0,)))
    for m, dst in enumerate(kvgrad):
        group = dst.shape[1]
        dst[0] = kgrad[m * group:(m + 1) * group].astype(jnp.bfloat16)
        dst[1] = vgrad[m * group:(m + 1) * group].astype(jnp.bfloat16)


def unpack_kernel(start, *refs):
    first, second = refs[8:]
    for m, ref in enumerate(refs[:8]):
        width = ref.shape[2]
        columns = pl.ds(pl.multiple_of(start[4 + m] * width, DH), width)
        first[:, columns] = ref[0]
        second[:, columns] = ref[1]


def video_kernel(kv0, kv1, kv2, kv3, qg, bias, kvg0, kvg1, kvg2, kvg3, oqgrad, probs_all, ds_all):
    width = kv0.shape[0] * kv0.shape[2]
    group = qg.shape[2]
    rows = qg.shape[0] * group
    query_all, cotan_all = rows_of(qg, 0), rows_of(qg, 1)
    refs = (kv0, kv1, kv2, kv3)
    keys = jnp.concatenate([rows_of(ref, 0) for ref in refs], axis=0)
    values = jnp.concatenate([rows_of(ref, 1) for ref in refs], axis=0)
    chunk = 256
    for start in range(0, rows, chunk):
        query = query_all[start:start + chunk]
        cotan = cotan_all[start:start + chunk]
        shift = jnp.concatenate([bias[...]] * (chunk // DH), axis=1)
        scores = mm(keys, query, ((1,), (1,))) * (SCALE * LOG2E) + shift
        peak = jnp.max(scores, axis=0, keepdims=True)
        raised = jnp.exp2(scores - peak)
        total = jnp.sum(raised, axis=0, keepdims=True)
        probs = raised * (1.0 / total)
        dprobs = mm(values, cotan, ((1,), (1,)))
        inner = jnp.sum(probs * dprobs, axis=0, keepdims=True)
        dscores = (probs * (dprobs - inner)).astype(jnp.bfloat16)
        probs = probs.astype(jnp.bfloat16)
        probs_all[:, start:start + chunk] = probs
        ds_all[:, start:start + chunk] = dscores
        out = mm(values, probs, ((0,), (0,)))
        qgrad = mm(keys, dscores, ((0,), (0,))) * SCALE
        at = pl.ds(start // group, chunk // group)
        shape = (chunk // group, group, DH)
        oqgrad[at, 0] = jnp.transpose(out).astype(jnp.bfloat16).reshape(shape)
        oqgrad[at, 1] = jnp.transpose(qgrad).astype(jnp.bfloat16).reshape(shape)
    kgrad = (mm(ds_all[...], query_all, ((1,), (0,))) * SCALE).astype(jnp.bfloat16)
    vgrad = mm(probs_all[...], cotan_all, ((1,), (0,))).astype(jnp.bfloat16)
    for block, dst in enumerate((kvg0, kvg1, kvg2, kvg3)):
        shape = (dst.shape[0], dst.shape[2], DH)
        dst[:, 0] = kgrad[block * width:(block + 1) * width].reshape(shape)
        dst[:, 1] = vgrad[block * width:(block + 1) * width].reshape(shape)


def head_block(shape, pair=0):
    block = (shape[0], 2) + tuple(shape[2:-1]) + (DH,)
    return pl.BlockSpec(block, lambda h: (0, pair, 0, h))


def sizes(blocks, video):
    tokens = len(blocks) * blocks[0].shape[0] * blocks[0].shape[2]
    return video.shape[0] * video.shape[2], tokens, video.shape[-1] // DH


def audio_stats(start, blocks, video):
    rows, tokens, heads = sizes(blocks, video)
    return pl.pallas_call(
        audio_stats_kernel,
        grid=(heads,),
        in_specs=[pl.BlockSpec(memory_space=pltpu.SMEM)]
        + [head_block(b.shape) for b in blocks]
        + [head_block(video.shape)],
        out_specs=pl.BlockSpec((1, 2, tokens), lambda h: (h, 0, 0)),
        out_shape=jax.ShapeDtypeStruct((heads, 2, tokens), jnp.float32),
        compiler_params=pltpu.CompilerParams(vmem_limit_bytes=VMEM),
        cost_estimate=LONG,
        name="audio_stats",
    )(start, *blocks, video)


def audio_grad(start, blocks, video, stats):
    rows, tokens, heads = sizes(blocks, video)
    part = jax.ShapeDtypeStruct((2,) + video.shape[2:], jnp.bfloat16)
    part_block = pl.BlockSpec(part.shape[:2] + (DH,), lambda h: (0, 0, h))
    block = jax.ShapeDtypeStruct(blocks[0].shape, jnp.bfloat16)
    result = pl.pallas_call(
        audio_grad_kernel,
        grid=(heads,),
        in_specs=[pl.BlockSpec(memory_space=pltpu.SMEM)]
        + [head_block(b.shape) for b in blocks]
        + [head_block(video.shape), pl.BlockSpec((1, 2, tokens), lambda h: (h, 0, 0))],
        out_specs=[head_block(b.shape) for b in blocks] + [part_block] * 8,
        out_shape=[block] * 4 + [part] * 8,
        scratch_shapes=[pltpu.VMEM((rows, tokens), jnp.bfloat16)] * 2,
        compiler_params=pltpu.CompilerParams(vmem_limit_bytes=VMEM),
        cost_estimate=LONG,
        name="audio_grad",
    )(start, *blocks, video, stats)
    return result[:4], result[4:]


def unpack(start, parts):
    _, rows, columns = parts[0].shape
    out = jax.ShapeDtypeStruct((rows, columns * 8), parts[0].dtype)
    in_vmem = pl.BlockSpec(memory_space=pltpu.VMEM)
    return pl.pallas_call(
        unpack_kernel,
        in_specs=[pl.BlockSpec(memory_space=pltpu.SMEM)] + [in_vmem] * 8,
        out_specs=[in_vmem] * 2,
        out_shape=[out] * 2,
        name="unpack",
    )(start, *parts)


def swap(parts):
    axes = ("xl", "zl", "core")
    masks = [(m & 1) * 4 + m // 2 for m in range(8)]
    return [parts[0]] + [
        lax.ppermute(parts[m], axes, [(i, i ^ masks[m]) for i in range(8)]) for m in range(1, 8)
    ]


def video_all(blocks, video, bias):
    rows, tokens, heads = sizes(blocks, video)
    pair = jax.ShapeDtypeStruct((video.shape[0], 2) + video.shape[2:], jnp.bfloat16)
    block = jax.ShapeDtypeStruct(blocks[0].shape, jnp.bfloat16)
    result = pl.pallas_call(
        video_kernel,
        grid=(heads,),
        in_specs=[head_block(b.shape) for b in blocks]
        + [head_block(video.shape, 1), pl.BlockSpec((tokens, DH), lambda h: (0, 0))],
        out_specs=[head_block(b.shape) for b in blocks] + [head_block(video.shape)],
        out_shape=[block] * 4 + [pair],
        scratch_shapes=[pltpu.VMEM((tokens, rows), jnp.bfloat16)] * 2,
        compiler_params=pltpu.CompilerParams(vmem_limit_bytes=VMEM),
        cost_estimate=LONG,
        name="video_all",
    )(*blocks, video, bias)
    return result[:4], result[4]


def exchange(x, axes):
    return lax.all_to_all(x, axes, split_axis=0, concat_axis=0)


def after(x, *others):
    return lax.optimization_barrier((x,) + others)[0]


def video_in(arrays, *others):
    rows, columns = arrays[0].shape
    stack = jnp.stack(arrays).reshape(len(arrays), rows, 8, columns // 8)
    return exchange(after(jnp.transpose(stack, (2, 0, 1, 3)), *others), HEADS8)


def video_out(pair, *others):
    back = jnp.transpose(exchange(after(pair, *others), HEADS8), (1, 2, 0, 3))
    back = back.reshape(2, back.shape[1], -1)
    return back[0], back[1]


def plane_in(arrays):
    stack = jnp.stack(arrays)
    half = stack.shape[-1] // 2
    halves = jnp.stack([stack[..., :half], stack[..., half:]])
    sends = jnp.broadcast_to(halves[None], (8,) + halves.shape)
    return exchange(sends.reshape((16,) + halves.shape[1:]), PLANE)


def plane_out(x, *others):
    got = exchange(after(x, *others), PLANE)
    got = got.reshape((8, 2) + got.shape[1:]).astype(jnp.float32).sum(axis=0)
    return jnp.concatenate([got[0], got[1]], axis=-1).astype(jnp.bfloat16)


def along_y(x, step):
    return lax.ppermute(x, "y", [(i, (i + step) % 4) for i in range(4)])


def gather_y(x):
    return [x] + [along_y(x, -step) for step in (1, 2, 3)]


def scatter_y(blocks):
    return [blocks[0]] + [along_y(blocks[step], step) for step in (1, 2, 3)]


def add(parts):
    return sum(part.astype(jnp.float32) for part in parts).astype(jnp.bfloat16)


def merge_stats(stats, axis):
    levels, means = stats
    top = jnp.max(levels, axis=axis, keepdims=True)
    weights = jnp.exp(levels - top)
    total = jnp.sum(weights, axis=axis, keepdims=True)
    mean = jnp.sum(weights * means, axis=axis, keepdims=True) / total
    return jnp.squeeze(top + jnp.log(total), axis), jnp.squeeze(mean, axis)


def per_device(
    video_query,
    video_key,
    video_value,
    video_cotan,
    audio_query,
    audio_key,
    audio_value,
    audio_cotan,
    alignment,
):
    y, zh = lax.axis_index("y"), lax.axis_index("zh")
    frame = y * 4 + zh
    tokens = alignment.shape[0]
    bias = -BIAS_SLOPE * jnp.abs(frame - alignment).astype(jnp.float32)
    start = ((y + jnp.arange(4, dtype=jnp.int32)) % 4) * (tokens // 4)
    place = lax.axis_index("zl") * 4 + lax.axis_index("core") * 2 + lax.axis_index("xl")
    start = jnp.concatenate([start, place ^ jnp.arange(8, dtype=jnp.int32)]).astype(jnp.int32)
    turned = lax.dynamic_slice_in_dim(jnp.tile(bias, 2), start[0], tokens)
    key_bias = jnp.broadcast_to((turned * LOG2E)[:, None], (tokens, DH))

    planes = plane_in([audio_query, audio_cotan, audio_key, audio_value])
    video = video_in([video_key, video_value, video_query, video_cotan], planes)
    audio_qg = gather_y(planes[:, :2])
    audio_kv = gather_y(after(planes[:, 2:], audio_qg[1], audio_qg[3]))

    stats = audio_stats(start, audio_qg, video)
    stats = after(jnp.stack([stats[:, 0] + bias, stats[:, 1]]), audio_kv[1], audio_kv[3])
    seen = jnp.stack(merge_stats(jnp.stack(gather_y(stats), axis=1), 0))
    key_bias = after(key_bias, seen)
    seen = exchange(jnp.broadcast_to(seen[None], (8,) + seen.shape), ("zh", "xh"))
    level, inner = merge_stats((seen[:, 0], seen[:, 1]), 0)
    stats = jnp.stack([level - bias, inner], axis=1)

    key_value_blocks, video_oq = video_all(audio_kv, video, key_bias)
    out_query_blocks, video_kvgrad = audio_grad(start, audio_qg, video, stats)

    parts = scatter_y(key_value_blocks)
    video_cross_output, video_query_grad = video_out(video_oq)
    gate = (video_query_grad,) + tuple(parts[1:])
    video_kvgrad = lax.optimization_barrier(tuple(video_kvgrad) + gate)[:8]
    video_kvgrad = swap(video_kvgrad)
    video_key_grad, video_value_grad = unpack(start, video_kvgrad)
    sums = plane_out(add(parts), video_query_grad, out_query_blocks[0])
    audio_key_grad, audio_value_grad = sums
    parts = scatter_y(out_query_blocks)
    parts = lax.optimization_barrier(tuple(parts) + tuple(video_kvgrad))[:4]
    sums = plane_out(add(parts), audio_key_grad)
    audio_cross_output, audio_query_grad = sums
    return (
        video_cross_output,
        audio_cross_output,
        video_query_grad,
        video_key_grad,
        video_value_grad,
        audio_query_grad,
        audio_key_grad,
        audio_value_grad,
    )


def solution(mesh):
    split = Mesh(mesh.devices.reshape(tuple(size for _, size in AXES)), NAMES)
    video = P(NAMES, None)
    audio = P(VID, AUD)
    return jax.shard_map(
        per_device,
        mesh=split,
        in_specs=(video,) * 4 + (audio,) * 4 + (P(),),
        out_specs=(video, audio, video, video, video, audio, audio, audio),
        check_vma=False,
    )
```

time: 1990 us -> 183 us (0.09)
  waiting for transfers between devices: 1070 us -> 58.4 us
  blocking collectives: 645 us -> 0 us
  starting transfers between devices: 143 us -> 77.5 us
  matrix products: 45.2 us -> 0 us
  local copies, waits for them, and re-layouts: 44.6 us -> 9.24 us
  Pallas kernels: 0 us -> 26.1 us
    reduce_scatter x3 -> x0, waiting for transfers between devices: 696 us -> none  [the longest x1 253 us: per_device(): lax.psum_scatter(akey_part, 'vid', scatter_dimension=0, tiled=True)]
    pmax x1 -> x0, blocking collectives: 323 us -> none  [per_device(): audio_peaks = lax.pmax(jnp.max(cross, axis=2), 'vid')]
    psum x1 -> x0, blocking collectives: 321 us -> none  [per_device(): full_out, audio_totals = lax.psum((partial_out, partial_totals), 'vid')]
    psum x1 -> x0, waiting for transfers between devices: 313 us -> none  [per_device(): full_out, audio_totals = lax.psum((partial_out, partial_totals), 'vid')]
    all_to_all x8 -> x6, starting transfers between devices: 143 us -> 46.4 us  [exchange(): return lax.all_to_all(x, axes, split_axis=0, concat_axis=0)]
    all_gather x4 -> x0, waiting for transfers between devices: 47.8 us -> none  [the longest x1 47.7 us: per_device(): lax.all_gather(audio_query, 'vid', axis=0, tiled=True)]
    dot_general x12 -> x0, matrix products: 45.2 us -> none  [the longest x1 6.23 us: per_device(): jnp.einsum('kbj,jky->bky', audio_raised.astype(jnp.bfloat16), vvalue_h, p...]
    ppermute x0 -> x22, starting transfers between devices: none -> 31.1 us  [the longest x15 21.3 us: along_y(): return lax.ppermute(x, 'y', [(i, (i + step) % 4) for i in range(4)])]
  transfers between devices with their start and end apart: 16 -> 28, of which waited for: 11 -> 9; matrix products, arithmetic and copies ran while one was open for 5% -> 6% of each run, Pallas kernels for 0% -> 14%
where the time goes in v1:
time: 183 us; the launch traced here: 182 us
  starting transfers between devices  77.5 us (42%)
  waiting for transfers between devices  58.4 us (32%)
  Pallas kernels  26.1 us (14%)
  local copies, waits for them, and re-layouts  9.24 us (5%)
  other arithmetic  9.22 us (5%)
    all_to_all x6, starting transfers between devices, exchange(): return lax.all_to_all(x, axes, split_axis=0, concat_axis=0)  46.4 us
    all_to_all x6, waiting for transfers between devices, exchange(): return lax.all_to_all(x, axes, split_axis=0, concat_axis=0)  32.3 us
    ppermute x15, starting transfers between devices, along_y(): return lax.ppermute(x, 'y', [(i, (i + step) % 4) for i in range(4)])  21.3 us
    ppermute x15, waiting for transfers between devices, along_y(): return lax.ppermute(x, 'y', [(i, (i + step) % 4) for i in range(4)])  16.3 us
    pallas_call x1, Pallas kernels, video_all(): pl.pallas_call(video_kernel, grid=(heads,), in_specs=[head_block(b.shape)...  10.5 us
    ppermute x7, waiting for transfers between devices, swap(): lax.ppermute(parts[m], axes, [(i, i ^ masks[m]) for i in range(8)])  9.77 us
    ppermute x7, starting transfers between devices, swap(): lax.ppermute(parts[m], axes, [(i, i ^ masks[m]) for i in range(8)])  9.75 us
    pallas_call x1, Pallas kernels, audio_grad(): pl.pallas_call(audio_grad_kernel, grid=(heads,), in_specs=[pl.BlockSpec(m...  8.27 us
  transfers between devices with their start and end apart: 28, of which 9 were waited for; matrix products, arithmetic and copies ran while one was open for 6% of the time, Pallas kernels for 14%

profile of v1, /device:TPU:33, one launch (start us, length us, event | category | flops | bytes accessed | tf_op | source)
XLA Modules:
  0.0 181.7 jit_solution(7985551506927298093)
XLA Ops:
  0.6 0.9 pad_maximum_fusion
  1.5 1.0 broadcast_in_dim.6
  2.5 10.0 %all-to-all-start = ((bf16[16,4,16,384]{3,2,1,0:T(8,128)(2,1)}), bf16[16,4,16,384]{3,2,1,0:T(8,128)(2,1)S(1)}, u32[]{:S(2)}, u32[]{:S(2)}) async-start(bf16[16,4,16,384]{3,2,1,0:T(8,128)(2,1)} %bitcast.6), calls=%async_computation | async-start | bytes 1572864 | tf_op jit(solution)/shard_map/all_to_all | solution.py:223
  12.8 0.7 copy-done.3
  13.8 1.4 maximum_bitcast_fusion
  15.2 19.8 %all-to-all-done = bf16[16,4,16,384]{3,2,1,0:T(8,128)(2,1)S(1)} async-done(((bf16[16,4,16,384]{3,2,1,0:T(8,128)(2,1)}), bf16[16,4,16,384]{3,2,1,0:T(8,128)(2,1)S(1)}, u32[]{:S(2)}, u32[]{:S(2)}) %all-to-all-start) | async-done | bytes 786464 | tf_op jit(solution)/shard_map/all_to_all | solution.py:223
  35.0 4.9 %all-to-all-start.1 = ((bf16[8,4,64,384]{3,2,1,0:T(8,128)(2,1)}), bf16[8,4,64,384]{3,2,1,0:T(8,128)(2,1)S(1)}, u32[]{:S(2)}, u32[]{:S(2)}) async-start(bf16[8,4,64,384]{3,2,1,0:T(8,128)(2,1)} %maximum_bitcast_fusion), calls=%async_computation.1 | async-start | bytes 3145728 | tf_op jit(solution)/shard_map/all_to_all | solution.py:223
  40.2 3.0 %collective-permute-start.5 = (bf16[16,2,16,384]{3,2,1,0:T(8,128)(2,1)S(1)}, bf16[16,2,16,384]{3,2,1,0:T(8,128)(2,1)S(1)}, u32[]{:S(2)}, u32[]{:S(2)}) collective-permute-start(bf16[16,2,16,384]{3,2,1,0:T(8,128)(2,1)S(1)} %get-tuple-element.88.qg0), channel_id=1, source_target_pairs={{0,128},{64,192},{128,0},{192,64},{1,129},{65,193},{129,1},{193,65... | collective-permute-start | bytes 1179656 | tf_op jit(solution)/shard_map/ppermute | solution.py:257
  43.6 2.3 %collective-permute-start = (bf16[16,2,16,384]{3,2,1,0:T(8,128)(2,1)S(1)}, bf16[16,2,16,384]{3,2,1,0:T(8,128)(2,1)}, u32[]{:S(2)}, u32[]{:S(2)}) collective-permute-start(bf16[16,2,16,384]{3,2,1,0:T(8,128)(2,1)S(1)} %get-tuple-element.88.qg0), channel_id=1, source_target_pairs={{0,192},{64,0},{128,64},{192,128},{1,193},{65,1},{129,65},{193,129... | collective-permute-start | bytes 1179656 | tf_op jit(solution)/shard_map/ppermute | solution.py:257
  46.5 14.7 %collective-permute-done.1.qg3 = bf16[16,2,16,384]{3,2,1,0:T(8,128)(2,1)S(1)} collective-permute-done((bf16[16,2,16,384]{3,2,1,0:T(8,128)(2,1)S(1)}, bf16[16,2,16,384]{3,2,1,0:T(8,128)(2,1)S(1)}, u32[]{:S(2)}, u32[]{:S(2)}) %collective-permute-start.1) | collective-permute-done | bytes 393248 | tf_op jit(solution)/shard_map/ppermute | solution.py:257
  61.3 1.4 collective-permute-start.4
  62.7 1.4 collective-permute-start.2
  64.9 1.2 copy-done
  66.0 5.2 %audio_stats.1 = f32[3,2,1024]{2,1,0:T(2,128)} custom-call(s32[12]{0:T(128)} %pad_add_fusion.start, bf16[16,2,16,384]{3,2,1,0:T(8,128)(2,1)} %copy-done.5, bf16[16,2,16,384]{3,2,1,0:T(8,128)(2,1)} %collective-permute-done.qg1, bf16[16,2,16,384]{3,2,1,0:T(8,128)(2,1)} %copy-done.17, bf16[16,2,16,384]{3,2,1,0:T(8,128)(2,1)} %copy-done.18, ...), custom_call_target="tpu_custom_call" | custom-call | flops 49999998976 | tf_op jit(solution)/shard_map/audio_stats/pallas_call | solution.py:147
  71.2 0.8 slice_bitcast_fusion.6
  71.9 0.8 fusion.14
  72.8 1.0 collective-permute-start.8
  73.8 2.3 %collective-permute-start.7 = (f32[2,3,1024]{2,0,1:T(2,128)S(1)}, f32[2,3,1024]{2,0,1:T(2,128)S(1)}, u32[]{:S(2)}, u32[]{:S(2)}) collective-permute-start(f32[2,3,1024]{2,0,1:T(2,128)S(1)} %pad_maximum_fusion.6), channel_id=1, source_target_pairs={{0,128},{64,192},{128,0},{192,64},{1,129},{65,193},{129,1},{193,65... | collective-permute-start | bytes 73736 | tf_op jit(solution)/shard_map/ppermute | solution.py:257
  76.1 1.2 collective-permute-start.6
  78.0 0.9 collective-permute-done.6
  79.3 1.0 broadcast_in_dim.7.bias
  80.3 0.8 broadcast_in_dim.8
  81.0 5.4 %all-to-all-start.3 = ((f32[8,2,3,1024]{3,1,2,0:T(2,128)}), f32[8,2,3,1024]{3,1,2,0:T(2,128)S(1)}, u32[]{:S(2)}, u32[]{:S(2)}) async-start(f32[8,2,3,1024]{3,1,2,0:T(2,128)} %broadcast_in_dim.8), calls=%async_computation.3 | async-start | bytes 393216 | tf_op jit(solution)/shard_map/all_to_all | solution.py:223
  87.0 0.7 copy-done.19
  87.8 10.5 %video_all.1 = (bf16[16,2,16,384]{3,2,1,0:T(8,128)(2,1)}, bf16[16,2,16,384]{3,2,1,0:T(8,128)(2,1)}, bf16[16,2,16,384]{3,2,1,0:T(8,128)(2,1)}, bf16[16,2,16,384]{3,2,1,0:T(8,128)(2,1)}, bf16[8,2,64,384]{3,2,1,0:T(8,128)(2,1)}) custom-call(bf16[16,2,16,384]{3,2,1,0:T(8,128)(2,1)} %copy-done.6, bf16[16,2,16,384]{3,2,1,0:T(8,128)(2,1)} %collective-permute-done.2.kv1, ...), custom_call_target="tpu_custom_call" | custom-call | flops 49999998976 | tf_op jit(solution)/shard_map/video_all/pallas_call | solution.py:207
  98.5 2.6 %collective-permute-start.13 = (bf16[16,2,16,384]{3,2,1,0:T(8,128)(2,1)}, bf16[16,2,16,384]{3,2,1,0:T(8,128)(2,1)S(1)}, u32[]{:S(2)}, u32[]{:S(2)}) collective-permute-start(bf16[16,2,16,384]{3,2,1,0:T(8,128)(2,1)} %get-tuple-element.63), channel_id=1, source_target_pairs={{0,128},{64,192},{128,0},{192,64},{1,129},{65,193},{129,1},{193,65... | collective-permute-start | bytes 1179656 | tf_op jit(solution)/shard_map/ppermute | solution.py:257
  101.7 7.8 %all-to-all-start.2 = ((bf16[8,2,64,384]{3,2,1,0:T(8,128)(2,1)}), bf16[8,2,64,384]{3,2,1,0:T(8,128)(2,1)S(1)}, u32[]{:S(2)}, u32[]{:S(2)}) async-start(bf16[8,2,64,384]{3,2,1,0:T(8,128)(2,1)} %get-tuple-element.49), calls=%async_computation.2 | async-start | bytes 1572864 | tf_op jit(solution)/shard_map/all_to_all | solution.py:223
  110.5 8.3 %audio_grad.1 = (bf16[16,2,16,384]{3,2,1,0:T(8,128)(2,1)}, bf16[16,2,16,384]{3,2,1,0:T(8,128)(2,1)}, bf16[16,2,16,384]{3,2,1,0:T(8,128)(2,1)}, bf16[16,2,16,384]...) custom-call(s32[12]{0:T(128)} %pad_add_fusion.start, ...), custom_call_target="tpu_custom_call" | custom-call | flops 49999998976 | tf_op jit(solution)/shard_map/audio_grad/pallas_call | solution.py:166
  118.8 1.8 %collective-permute-start.9 = (bf16[16,2,16,384]{3,2,1,0:T(8,128)(2,1)}, bf16[16,2,16,384]{3,2,1,0:T(8,128)(2,1)S(1)}, u32[]{:S(2)}, u32[]{:S(2)}) collective-permute-start(bf16[16,2,16,384]{3,2,1,0:T(8,128)(2,1)} %get-tuple-element.51), channel_id=1, source_target_pairs={{0,64},{64,128},{128,192},{192,0},{1,65},{65,129},{129,193},{193,1... | collective-permute-start | bytes 1179656 | tf_op jit(solution)/shard_map/ppermute | solution.py:257
  120.9 2.2 %collective-permute-start.11 = (bf16[16,2,16,384]{3,2,1,0:T(8,128)(2,1)}, bf16[16,2,16,384]{3,2,1,0:T(8,128)(2,1)S(1)}, u32[]{:S(2)}, u32[]{:S(2)}) collective-permute-start(bf16[16,2,16,384]{3,2,1,0:T(8,128)(2,1)} %get-tuple-element.53), channel_id=1, source_target_pairs={{0,192},{64,0},{128,64},{192,128},{1,193},{65,1},{129,65},{193,129... | collective-permute-start | bytes 1179656 | tf_op jit(solution)/shard_map/ppermute | solution.py:257
  123.1 1.9 %add_convert_fusion = bf16[16,2,16,384]{3,2,1,0:T(8,128)(2,1)} fusion(bf16[16,2,16,384]{3,2,1,0:T(8,128)(2,1)} %collective-permute-done.14, bf16[16,2,16,384]{3,2,1,0:T(8,128)(2,1)S(1)} %collective-permute-done.13, bf16[16,2,16,384]{3,2,1,0:T(8,128)(2,1)S(1)} %collective-permute-done.12, bf16[16,2,16,384]{3,2,1,0:T(8,128)(2,1)S(1)} %copy-done.8), kind=kLoop, calls=%fused_computation.1 | loop fusion | flops 1572864 | bytes 1966080 | tf_op jit(solution)/shard_map/convert_element_type | solution.py:269
  125.2 0.8 copy.72
  126.0 9.8 %all-to-all-start.4 = ((bf16[16,2,16,384]{3,2,1,0:T(8,128)(2,1)}), bf16[16,2,16,384]{3,2,1,0:T(8,128)(2,1)S(1)}, u32[]{:S(2)}, u32[]{:S(2)}) async-start(bf16[16,2,16,384]{3,2,1,0:T(8,128)(2,1)} %add_convert_fusion), calls=%async_computation.4 | async-start | bytes 786432 | tf_op jit(solution)/shard_map/all_to_all | solution.py:223
  135.8 1.4 collective-permute-start.15
  137.2 1.7 collective-permute-start.16
  139.0 2.3 %collective-permute-start.17 = (bf16[2,64,384]{2,1,0:T(8,128)(2,1)S(1)}, bf16[2,64,384]{2,1,0:T(8,128)(2,1)S(1)}, u32[]{:S(2)}, u32[]{:S(2)}) collective-permute-start(bf16[2,64,384]{2,1,0:T(8,128)(2,1)S(1)} %copy-done.24), channel_id=1, source_target_pairs={{0,5},{1,4},{2,7},{3,6},{4,1},{5,0},{6,3},{7,2},{8,13},{9,12},{10,... | collective-permute-start | bytes 294920 | tf_op jit(solution)/shard_map/ppermute | solution.py:199
  141.6 1.2 collective-permute-start.19
  142.8 0.7 collective-permute-start.20
  143.5 2.1 %collective-permute-start.21 = (bf16[2,64,384]{2,1,0:T(8,128)(2,1)S(1)}, bf16[2,64,384]{2,1,0:T(8,128)(2,1)S(1)}, u32[]{:S(2)}, u32[]{:S(2)}) collective-permute-start(bf16[2,64,384]{2,1,0:T(8,128)(2,1)S(1)} %copy-done.20), channel_id=1, source_target_pairs={{0,7},{1,6},{2,5},{3,4},{4,3},{5,2},{6,1},{7,0},{8,15},{9,14},{10,... | collective-permute-start | bytes 294920 | tf_op jit(solution)/shard_map/ppermute | solution.py:199
  145.6 3.5 %collective-permute-done.18.refs_4_ = bf16[2,64,384]{2,1,0:T(8,128)(2,1)S(1)} collective-permute-done((bf16[2,64,384]{2,1,0:T(8,128)(2,1)S(1)}, bf16[2,64,384]{2,1,0:T(8,128)(2,1)S(1)}, u32[]{:S(2)}, u32[]{:S(2)}) %collective-permute-start.18) | collective-permute-done | bytes 98336 | tf_op jit(solution)/shard_map/ppermute | solution.py:199
  149.1 2.1 %collective-permute-done.19.refs_5_ = bf16[2,64,384]{2,1,0:T(8,128)(2,1)S(1)} collective-permute-done((bf16[2,64,384]{2,1,0:T(8,128)(2,1)S(1)}, bf16[2,64,384]{2,1,0:T(8,128)(2,1)S(1)}, u32[]{:S(2)}, u32[]{:S(2)}) %collective-permute-start.19) | collective-permute-done | bytes 98336 | tf_op jit(solution)/shard_map/ppermute | solution.py:199
  151.1 1.5 collective-permute-done.20.refs_6_
  152.7 2.7 %collective-permute-done.21.refs_7_ = bf16[2,64,384]{2,1,0:T(8,128)(2,1)S(1)} collective-permute-done((bf16[2,64,384]{2,1,0:T(8,128)(2,1)S(1)}, bf16[2,64,384]{2,1,0:T(8,128)(2,1)S(1)}, u32[]{:S(2)}, u32[]{:S(2)}) %collective-permute-start.21) | collective-permute-done | bytes 98336 | tf_op jit(solution)/shard_map/ppermute | solution.py:199
  155.4 1.0 add_convert_fusion.1
  157.1 8.5 %all-to-all-start.5 = ((bf16[16,2,16,384]{3,2,1,0:T(8,128)(2,1)}), bf16[16,2,16,384]{3,2,1,0:T(8,128)(2,1)S(1)}, u32[]{:S(2)}, u32[]{:S(2)}) async-start(bf16[16,2,16,384]{3,2,1,0:T(8,128)(2,1)} %add_convert_fusion.1), calls=%async_computation.5 | async-start | bytes 786432 | tf_op jit(solution)/shard_map/all_to_all | solution.py:223
  165.6 0.8 copy.71
  166.4 2.2 %unpack.1 = (bf16[64,3072]{1,0:T(8,128)(2,1)}, bf16[64,3072]{1,0:T(8,128)(2,1)}) custom-call(s32[12]{0:T(128)} %pad_add_fusion.start, bf16[2,64,384]{2,1,0:T(8,128)(2,1)} %get-tuple-element.65.refs_0_, bf16[2,64,384]{2,1,0:T(8,128)(2,1)} %copy-done.9, bf16[2,64,384]{2,1,0:T(8,128)(2,1)} %copy-done.10, bf16[2,64,384]{2,1,0:T(8,128)(2,1)} %copy-done.11, ...), custom_call_target="tpu_custom_call" | custom-call | tf_op jit(solution)/shard_map/unpack/pallas_call | solution.py:186
  168.5 12.5 %all-to-all-done.5 = bf16[16,2,16,384]{3,2,1,0:T(8,128)(2,1)S(1)} async-done(((bf16[16,2,16,384]{3,2,1,0:T(8,128)(2,1)}), bf16[16,2,16,384]{3,2,1,0:T(8,128)(2,1)S(1)}, u32[]{:S(2)}, u32[]{:S(2)}) %all-to-all-start.5) | async-done | bytes 393248 | tf_op jit(solution)/shard_map/all_to_all | solution.py:223
  (116 shorter events, 7.9 us)
Async XLA Ops:
  0.6 11.9 %copy-start.1 = (bf16[64,3072]{1,0:T(8,128)(2,1)S(1)}, bf16[64,3072]{1,0:T(8,128)(2,1)}, u32[]{:S(2)}) copy-start(bf16[64,3072]{1,0:T(8,128)(2,1)} %param.9) | copy-start | bytes 1179652
  2.5 10.1 %copy-start.2 = (bf16[64,3072]{1,0:T(8,128)(2,1)S(1)}, bf16[64,3072]{1,0:T(8,128)(2,1)}, u32[]{:S(2)}) copy-start(bf16[64,3072]{1,0:T(8,128)(2,1)} %param.10) | copy-start | bytes 1179652
  2.5 32.5 %all-to-all-start = ((bf16[16,4,16,384]{3,2,1,0:T(8,128)(2,1)}), bf16[16,4,16,384]{3,2,1,0:T(8,128)(2,1)S(1)}, u32[]{:S(2)}, u32[]{:S(2)}) async-start(bf16[16,4,16,384]{3,2,1,0:T(8,128)(2,1)} %bitcast.6), calls=%async_computation | async-start | bytes 1572864 | tf_op jit(solution)/shard_map/all_to_all | solution.py:223
  15.2 24.8 %copy-start.16 = (s32[1024]{0:T(1024)S(1)}, s32[1024]{0:T(1024)}, u32[]{:S(2)}) copy-start(s32[1024]{0:T(1024)} %param.17) | copy-start | bytes 12292
  35.0 29.1 %all-to-all-start.1 = ((bf16[8,4,64,384]{3,2,1,0:T(8,128)(2,1)}), bf16[8,4,64,384]{3,2,1,0:T(8,128)(2,1)S(1)}, u32[]{:S(2)}, u32[]{:S(2)}) async-start(bf16[8,4,64,384]{3,2,1,0:T(8,128)(2,1)} %maximum_bitcast_fusion), calls=%async_computation.1 | async-start | bytes 3145728 | tf_op jit(solution)/shard_map/all_to_all | solution.py:223
  40.2 23.9 %copy-start.5 = (bf16[16,2,16,384]{3,2,1,0:T(8,128)(2,1)}, bf16[16,2,16,384]{3,2,1,0:T(8,128)(2,1)S(1)}, u32[]{:S(2)}) copy-start(bf16[16,2,16,384]{3,2,1,0:T(8,128)(2,1)S(1)} %get-tuple-element.88.qg0) | copy-start | bytes 1179652
  40.2 37.2 %copy-start.6 = (bf16[16,2,16,384]{3,2,1,0:T(8,128)(2,1)}, bf16[16,2,16,384]{3,2,1,0:T(8,128)(2,1)S(1)}, u32[]{:S(2)}) copy-start(bf16[16,2,16,384]{3,2,1,0:T(8,128)(2,1)S(1)} %get-tuple-element.45.kv0) | copy-start | bytes 1179652
  40.2 23.9 %collective-permute-start.5 = (bf16[16,2,16,384]{3,2,1,0:T(8,128)(2,1)S(1)}, bf16[16,2,16,384]{3,2,1,0:T(8,128)(2,1)S(1)}, u32[]{:S(2)}, u32[]{:S(2)}) collective-permute-start(bf16[16,2,16,384]{3,2,1,0:T(8,128)(2,1)S(1)} %get-tuple-element.88.qg0), channel_id=1, source_target_pairs={{0,128},{64,192},{128,0},{192,64},{1,129},{65,193},{129,1},{193,65... | collective-permute-start | bytes 1179656 | tf_op jit(solution)/shard_map/ppermute | solution.py:257
  43.2 18.1 %collective-permute-start.1 = (bf16[16,2,16,384]{3,2,1,0:T(8,128)(2,1)S(1)}, bf16[16,2,16,384]{3,2,1,0:T(8,128)(2,1)S(1)}, u32[]{:S(2)}, u32[]{:S(2)}) collective-permute-start(bf16[16,2,16,384]{3,2,1,0:T(8,128)(2,1)S(1)} %get-tuple-element.88.qg0), channel_id=1, source_target_pairs={{0,64},{64,128},{128,192},{192,0},{1,65},{65,129},{129,193},{193,1... | collective-permute-start | bytes 1179656 | tf_op jit(solution)/shard_map/ppermute | solution.py:257
  43.6 17.7 %collective-permute-start = (bf16[16,2,16,384]{3,2,1,0:T(8,128)(2,1)S(1)}, bf16[16,2,16,384]{3,2,1,0:T(8,128)(2,1)}, u32[]{:S(2)}, u32[]{:S(2)}) collective-permute-start(bf16[16,2,16,384]{3,2,1,0:T(8,128)(2,1)S(1)} %get-tuple-element.88.qg0), channel_id=1, source_target_pairs={{0,192},{64,0},{128,64},{192,128},{1,193},{65,1},{129,65},{193,129... | collective-permute-start | bytes 1179656 | tf_op jit(solution)/shard_map/ppermute | solution.py:257
  61.3 11.5 %collective-permute-start.4 = (bf16[16,2,16,384]{3,2,1,0:T(8,128)(2,1)S(1)}, bf16[16,2,16,384]{3,2,1,0:T(8,128)(2,1)}, u32[]{:S(2)}, u32[]{:S(2)}) collective-permute-start(bf16[16,2,16,384]{3,2,1,0:T(8,128)(2,1)S(1)} %get-tuple-element.45.kv0), channel_id=1, source_target_pairs={{0,64},{64,128},{128,192},{192,0},{1,65},{65,129},{129,193},{193,1... | collective-permute-start | bytes 1179656 | tf_op jit(solution)/shard_map/ppermute | solution.py:257
  62.7 10.1 %collective-permute-start.2 = (bf16[16,2,16,384]{3,2,1,0:T(8,128)(2,1)S(1)}, bf16[16,2,16,384]{3,2,1,0:T(8,128)(2,1)}, u32[]{:S(2)}, u32[]{:S(2)}) collective-permute-start(bf16[16,2,16,384]{3,2,1,0:T(8,128)(2,1)S(1)} %get-tuple-element.45.kv0), channel_id=1, source_target_pairs={{0,192},{64,0},{128,64},{192,128},{1,193},{65,1},{129,65},{193,129... | collective-permute-start | bytes 1179656 | tf_op jit(solution)/shard_map/ppermute | solution.py:257
  72.8 5.2 %collective-permute-start.8 = (f32[2,3,1024]{2,0,1:T(2,128)S(1)}, f32[2,3,1024]{2,0,1:T(2,128)S(1)}, u32[]{:S(2)}, u32[]{:S(2)}) collective-permute-start(f32[2,3,1024]{2,0,1:T(2,128)S(1)} %pad_maximum_fusion.6), channel_id=1, source_target_pairs={{0,64},{64,128},{128,192},{192,0},{1,65},{65,129},{129,193},{193,1... | collective-permute-start | bytes 73736 | tf_op jit(solution)/shard_map/ppermute | solution.py:257
  73.8 4.2 %collective-permute-start.7 = (f32[2,3,1024]{2,0,1:T(2,128)S(1)}, f32[2,3,1024]{2,0,1:T(2,128)S(1)}, u32[]{:S(2)}, u32[]{:S(2)}) collective-permute-start(f32[2,3,1024]{2,0,1:T(2,128)S(1)} %pad_maximum_fusion.6), channel_id=1, source_target_pairs={{0,128},{64,192},{128,0},{192,64},{1,129},{65,193},{129,1},{193,65... | collective-permute-start | bytes 73736 | tf_op jit(solution)/shard_map/ppermute | solution.py:257
  76.1 2.8 %collective-permute-start.6 = (f32[2,3,1024]{2,0,1:T(2,128)S(1)}, f32[2,3,1024]{2,0,1:T(2,128)S(1)}, u32[]{:S(2)}, u32[]{:S(2)}) collective-permute-start(f32[2,3,1024]{2,0,1:T(2,128)S(1)} %pad_maximum_fusion.6), channel_id=1, source_target_pairs={{0,192},{64,0},{128,64},{192,128},{1,193},{65,1},{129,65},{193,129... | collective-permute-start | bytes 73736 | tf_op jit(solution)/shard_map/ppermute | solution.py:257
  77.4 9.6 %collective-permute-start.3 = (bf16[16,2,16,384]{3,2,1,0:T(8,128)(2,1)S(1)}, bf16[16,2,16,384]{3,2,1,0:T(8,128)(2,1)S(1)}, u32[]{:S(2)}, u32[]{:S(2)}) collective-permute-start(bf16[16,2,16,384]{3,2,1,0:T(8,128)(2,1)S(1)} %get-tuple-element.45.kv0), channel_id=1, source_target_pairs={{0,128},{64,192},{128,0},{192,64},{1,129},{65,193},{129,1},{193,65... | collective-permute-start | bytes 1179656 | tf_op jit(solution)/shard_map/ppermute | solution.py:257
  81.0 20.6 %all-to-all-start.3 = ((f32[8,2,3,1024]{3,1,2,0:T(2,128)}), f32[8,2,3,1024]{3,1,2,0:T(2,128)S(1)}, u32[]{:S(2)}, u32[]{:S(2)}) async-start(f32[8,2,3,1024]{3,1,2,0:T(2,128)} %broadcast_in_dim.8), calls=%async_computation.3 | async-start | bytes 393216 | tf_op jit(solution)/shard_map/all_to_all | solution.py:223
  98.3 22.6 %collective-permute-start.12 = (bf16[16,2,16,384]{3,2,1,0:T(8,128)(2,1)}, bf16[16,2,16,384]{3,2,1,0:T(8,128)(2,1)S(1)}, u32[]{:S(2)}, u32[]{:S(2)}) collective-permute-start(bf16[16,2,16,384]{3,2,1,0:T(8,128)(2,1)} %get-tuple-element.62), channel_id=1, source_target_pairs={{0,64},{64,128},{128,192},{192,0},{1,65},{65,129},{129,193},{193,1... | collective-permute-start | bytes 1179656 | tf_op jit(solution)/shard_map/ppermute | solution.py:257
  98.5 24.5 %collective-permute-start.13 = (bf16[16,2,16,384]{3,2,1,0:T(8,128)(2,1)}, bf16[16,2,16,384]{3,2,1,0:T(8,128)(2,1)S(1)}, u32[]{:S(2)}, u32[]{:S(2)}) collective-permute-start(bf16[16,2,16,384]{3,2,1,0:T(8,128)(2,1)} %get-tuple-element.63), channel_id=1, source_target_pairs={{0,128},{64,192},{128,0},{192,64},{1,129},{65,193},{129,1},{193,65... | collective-permute-start | bytes 1179656 | tf_op jit(solution)/shard_map/ppermute | solution.py:257
  101.1 22.0 %collective-permute-start.14 = (bf16[16,2,16,384]{3,2,1,0:T(8,128)(2,1)}, bf16[16,2,16,384]{3,2,1,0:T(8,128)(2,1)}, u32[]{:S(2)}, u32[]{:S(2)}) collective-permute-start(bf16[16,2,16,384]{3,2,1,0:T(8,128)(2,1)} %get-tuple-element.64), channel_id=1, source_target_pairs={{0,192},{64,0},{128,64},{192,128},{1,193},{65,1},{129,65},{193,129... | collective-permute-start | bytes 1179656 | tf_op jit(solution)/shard_map/ppermute | solution.py:257
  101.7 23.4 %all-to-all-start.2 = ((bf16[8,2,64,384]{3,2,1,0:T(8,128)(2,1)}), bf16[8,2,64,384]{3,2,1,0:T(8,128)(2,1)S(1)}, u32[]{:S(2)}, u32[]{:S(2)}) async-start(bf16[8,2,64,384]{3,2,1,0:T(8,128)(2,1)} %get-tuple-element.49), calls=%async_computation.2 | async-start | bytes 1572864 | tf_op jit(solution)/shard_map/all_to_all | solution.py:223
  110.5 12.6 %copy-start.8 = (bf16[16,2,16,384]{3,2,1,0:T(8,128)(2,1)S(1)}, bf16[16,2,16,384]{3,2,1,0:T(8,128)(2,1)}, u32[]{:S(2)}) copy-start(bf16[16,2,16,384]{3,2,1,0:T(8,128)(2,1)} %get-tuple-element.77) | copy-start | bytes 1179652
  118.8 20.2 %collective-permute-start.9 = (bf16[16,2,16,384]{3,2,1,0:T(8,128)(2,1)}, bf16[16,2,16,384]{3,2,1,0:T(8,128)(2,1)S(1)}, u32[]{:S(2)}, u32[]{:S(2)}) collective-permute-start(bf16[16,2,16,384]{3,2,1,0:T(8,128)(2,1)} %get-tuple-element.51), channel_id=1, source_target_pairs={{0,64},{64,128},{128,192},{192,0},{1,65},{65,129},{129,193},{193,1... | collective-permute-start | bytes 1179656 | tf_op jit(solution)/shard_map/ppermute | solution.py:257
  120.6 20.7 %collective-permute-start.10 = (bf16[16,2,16,384]{3,2,1,0:T(8,128)(2,1)}, bf16[16,2,16,384]{3,2,1,0:T(8,128)(2,1)S(1)}, u32[]{:S(2)}, u32[]{:S(2)}) collective-permute-start(bf16[16,2,16,384]{3,2,1,0:T(8,128)(2,1)} %get-tuple-element.52), channel_id=1, source_target_pairs={{0,128},{64,192},{128,0},{192,64},{1,129},{65,193},{129,1},{193,65... | collective-permute-start | bytes 1179656 | tf_op jit(solution)/shard_map/ppermute | solution.py:257
  120.9 20.6 %collective-permute-start.11 = (bf16[16,2,16,384]{3,2,1,0:T(8,128)(2,1)}, bf16[16,2,16,384]{3,2,1,0:T(8,128)(2,1)S(1)}, u32[]{:S(2)}, u32[]{:S(2)}) collective-permute-start(bf16[16,2,16,384]{3,2,1,0:T(8,128)(2,1)} %get-tuple-element.53), channel_id=1, source_target_pairs={{0,192},{64,0},{128,64},{192,128},{1,193},{65,1},{129,65},{193,129... | collective-permute-start | bytes 1179656 | tf_op jit(solution)/shard_map/ppermute | solution.py:257
  125.0 16.2 %copy-start.23 = (bf16[2,64,384]{2,1,0:T(8,128)(2,1)S(1)}, bf16[2,64,384]{2,1,0:T(8,128)(2,1)}, u32[]{:S(2)}) copy-start(bf16[2,64,384]{2,1,0:T(8,128)(2,1)} %get-tuple-element.69) | copy-start | bytes 294916
  125.0 16.5 %copy-start.22 = (bf16[2,64,384]{2,1,0:T(8,128)(2,1)S(1)}, bf16[2,64,384]{2,1,0:T(8,128)(2,1)}, u32[]{:S(2)}) copy-start(bf16[2,64,384]{2,1,0:T(8,128)(2,1)} %get-tuple-element.70) | copy-start | bytes 294916
  125.0 17.7 %copy-start.21 = (bf16[2,64,384]{2,1,0:T(8,128)(2,1)S(1)}, bf16[2,64,384]{2,1,0:T(8,128)(2,1)}, u32[]{:S(2)}) copy-start(bf16[2,64,384]{2,1,0:T(8,128)(2,1)} %get-tuple-element.71) | copy-start | bytes 294916
  125.1 18.5 %copy-start.20 = (bf16[2,64,384]{2,1,0:T(8,128)(2,1)S(1)}, bf16[2,64,384]{2,1,0:T(8,128)(2,1)}, u32[]{:S(2)}) copy-start(bf16[2,64,384]{2,1,0:T(8,128)(2,1)} %get-tuple-element.72) | copy-start | bytes 294916
  125.1 30.3 %copy-start.7 = (bf16[16,2,16,384]{3,2,1,0:T(8,128)(2,1)S(1)}, bf16[16,2,16,384]{3,2,1,0:T(8,128)(2,1)}, u32[]{:S(2)}) copy-start(bf16[16,2,16,384]{3,2,1,0:T(8,128)(2,1)} %get-tuple-element.73) | copy-start | bytes 1179652
  125.2 10.6 %copy-start.26 = (bf16[2,64,384]{2,1,0:T(8,128)(2,1)S(1)}, bf16[2,64,384]{2,1,0:T(8,128)(2,1)}, u32[]{:S(2)}) copy-start(bf16[2,64,384]{2,1,0:T(8,128)(2,1)} %get-tuple-element.66) | copy-start | bytes 294916
  125.2 12.1 %copy-start.25 = (bf16[2,64,384]{2,1,0:T(8,128)(2,1)S(1)}, bf16[2,64,384]{2,1,0:T(8,128)(2,1)}, u32[]{:S(2)}) copy-start(bf16[2,64,384]{2,1,0:T(8,128)(2,1)} %get-tuple-element.67) | copy-start | bytes 294916
  125.2 13.8 %copy-start.24 = (bf16[2,64,384]{2,1,0:T(8,128)(2,1)S(1)}, bf16[2,64,384]{2,1,0:T(8,128)(2,1)}, u32[]{:S(2)}) copy-start(bf16[2,64,384]{2,1,0:T(8,128)(2,1)} %get-tuple-element.68) | copy-start | bytes 294916
  126.0 30.3 %all-to-all-start.4 = ((bf16[16,2,16,384]{3,2,1,0:T(8,128)(2,1)}), bf16[16,2,16,384]{3,2,1,0:T(8,128)(2,1)S(1)}, u32[]{:S(2)}, u32[]{:S(2)}) async-start(bf16[16,2,16,384]{3,2,1,0:T(8,128)(2,1)} %add_convert_fusion), calls=%async_computation.4 | async-start | bytes 786432 | tf_op jit(solution)/shard_map/all_to_all | solution.py:223
  135.8 7.0 %collective-permute-start.15 = (bf16[2,64,384]{2,1,0:T(8,128)(2,1)S(1)}, bf16[2,64,384]{2,1,0:T(8,128)(2,1)S(1)}, u32[]{:S(2)}, u32[]{:S(2)}) collective-permute-start(bf16[2,64,384]{2,1,0:T(8,128)(2,1)S(1)} %copy-done.26), channel_id=1, source_target_pairs={{0,4},{1,5},{2,6},{3,7},{4,0},{5,1},{6,2},{7,3},{8,12},{9,13},{10,... | collective-permute-start | bytes 294920 | tf_op jit(solution)/shard_map/ppermute | solution.py:199
  137.2 6.3 %collective-permute-start.16 = (bf16[2,64,384]{2,1,0:T(8,128)(2,1)S(1)}, bf16[2,64,384]{2,1,0:T(8,128)(2,1)S(1)}, u32[]{:S(2)}, u32[]{:S(2)}) collective-permute-start(bf16[2,64,384]{2,1,0:T(8,128)(2,1)S(1)} %copy-done.25), channel_id=1, source_target_pairs={{0,1},{1,0},{2,3},{3,2},{4,5},{5,4},{6,7},{7,6},{8,9},{9,8},{10,11... | collective-permute-start | bytes 294920 | tf_op jit(solution)/shard_map/ppermute | solution.py:199
  139.0 6.6 %collective-permute-start.17 = (bf16[2,64,384]{2,1,0:T(8,128)(2,1)S(1)}, bf16[2,64,384]{2,1,0:T(8,128)(2,1)S(1)}, u32[]{:S(2)}, u32[]{:S(2)}) collective-permute-start(bf16[2,64,384]{2,1,0:T(8,128)(2,1)S(1)} %copy-done.24), channel_id=1, source_target_pairs={{0,5},{1,4},{2,7},{3,6},{4,1},{5,0},{6,3},{7,2},{8,13},{9,12},{10,... | collective-permute-start | bytes 294920 | tf_op jit(solution)/shard_map/ppermute | solution.py:199
  141.3 7.8 %collective-permute-start.18 = (bf16[2,64,384]{2,1,0:T(8,128)(2,1)S(1)}, bf16[2,64,384]{2,1,0:T(8,128)(2,1)S(1)}, u32[]{:S(2)}, u32[]{:S(2)}) collective-permute-start(bf16[2,64,384]{2,1,0:T(8,128)(2,1)S(1)} %copy-done.23), channel_id=1, source_target_pairs={{0,2},{1,3},{2,0},{3,1},{4,6},{5,7},{6,4},{7,5},{8,10},{9,11},{10,... | collective-permute-start | bytes 294920 | tf_op jit(solution)/shard_map/ppermute | solution.py:199
  141.6 9.6 %collective-permute-start.19 = (bf16[2,64,384]{2,1,0:T(8,128)(2,1)S(1)}, bf16[2,64,384]{2,1,0:T(8,128)(2,1)S(1)}, u32[]{:S(2)}, u32[]{:S(2)}) collective-permute-start(bf16[2,64,384]{2,1,0:T(8,128)(2,1)S(1)} %copy-done.22), channel_id=1, source_target_pairs={{0,6},{1,7},{2,4},{3,5},{4,2},{5,3},{6,0},{7,1},{8,14},{9,15},{10,... | collective-permute-start | bytes 294920 | tf_op jit(solution)/shard_map/ppermute | solution.py:199
  142.8 14.3 %copy-start.9 = (bf16[2,64,384]{2,1,0:T(8,128)(2,1)}, bf16[2,64,384]{2,1,0:T(8,128)(2,1)S(1)}, u32[]{:S(2)}) copy-start(bf16[2,64,384]{2,1,0:T(8,128)(2,1)S(1)} %collective-permute-done.15.refs_1_) | copy-start | bytes 294916
  142.8 9.9 %collective-permute-start.20 = (bf16[2,64,384]{2,1,0:T(8,128)(2,1)S(1)}, bf16[2,64,384]{2,1,0:T(8,128)(2,1)S(1)}, u32[]{:S(2)}, u32[]{:S(2)}) collective-permute-start(bf16[2,64,384]{2,1,0:T(8,128)(2,1)S(1)} %copy-done.21), channel_id=1, source_target_pairs={{0,3},{1,2},{2,1},{3,0},{4,7},{5,6},{6,5},{7,4},{8,11},{9,10},{10,... | collective-permute-start | bytes 294920 | tf_op jit(solution)/shard_map/ppermute | solution.py:199
  143.5 13.5 %copy-start.10 = (bf16[2,64,384]{2,1,0:T(8,128)(2,1)}, bf16[2,64,384]{2,1,0:T(8,128)(2,1)S(1)}, u32[]{:S(2)}) copy-start(bf16[2,64,384]{2,1,0:T(8,128)(2,1)S(1)} %collective-permute-done.16.refs_2_) | copy-start | bytes 294916
  143.5 11.8 %collective-permute-start.21 = (bf16[2,64,384]{2,1,0:T(8,128)(2,1)S(1)}, bf16[2,64,384]{2,1,0:T(8,128)(2,1)S(1)}, u32[]{:S(2)}, u32[]{:S(2)}) collective-permute-start(bf16[2,64,384]{2,1,0:T(8,128)(2,1)S(1)} %copy-done.20), channel_id=1, source_target_pairs={{0,7},{1,6},{2,5},{3,4},{4,3},{5,2},{6,1},{7,0},{8,15},{9,14},{10,... | collective-permute-start | bytes 294920 | tf_op jit(solution)/shard_map/ppermute | solution.py:199
  145.6 11.4 %copy-start.11 = (bf16[2,64,384]{2,1,0:T(8,128)(2,1)}, bf16[2,64,384]{2,1,0:T(8,128)(2,1)S(1)}, u32[]{:S(2)}) copy-start(bf16[2,64,384]{2,1,0:T(8,128)(2,1)S(1)} %collective-permute-done.17.refs_3_) | copy-start | bytes 294916
  149.1 8.0 %copy-start.12 = (bf16[2,64,384]{2,1,0:T(8,128)(2,1)}, bf16[2,64,384]{2,1,0:T(8,128)(2,1)S(1)}, u32[]{:S(2)}) copy-start(bf16[2,64,384]{2,1,0:T(8,128)(2,1)S(1)} %collective-permute-done.18.refs_4_) | copy-start | bytes 294916
  151.1 5.9 %copy-start.13 = (bf16[2,64,384]{2,1,0:T(8,128)(2,1)}, bf16[2,64,384]{2,1,0:T(8,128)(2,1)S(1)}, u32[]{:S(2)}) copy-start(bf16[2,64,384]{2,1,0:T(8,128)(2,1)S(1)} %collective-permute-done.19.refs_5_) | copy-start | bytes 294916
  152.7 4.4 %copy-start.14 = (bf16[2,64,384]{2,1,0:T(8,128)(2,1)}, bf16[2,64,384]{2,1,0:T(8,128)(2,1)S(1)}, u32[]{:S(2)}) copy-start(bf16[2,64,384]{2,1,0:T(8,128)(2,1)S(1)} %collective-permute-done.20.refs_6_) | copy-start | bytes 294916
  157.1 23.9 %all-to-all-start.5 = ((bf16[16,2,16,384]{3,2,1,0:T(8,128)(2,1)}), bf16[16,2,16,384]{3,2,1,0:T(8,128)(2,1)S(1)}, u32[]{:S(2)}, u32[]{:S(2)}) async-start(bf16[16,2,16,384]{3,2,1,0:T(8,128)(2,1)} %add_convert_fusion.1), calls=%async_computation.5 | async-start | bytes 786432 | tf_op jit(solution)/shard_map/all_to_all | solution.py:223
  (7 other events, 9.3 us)

commit v2 on v1

--- a/solution.py
+++ b/solution.py
@@ -51,11 +51,10 @@
 
 
 def audio_grad_kernel(
-    start, qg0, qg1, qg2, qg3, kv, stats, od0, od1, od2, od3, *refs
+    start, qg0, qg1, qg2, qg3, kv, stats, video_grads, od0, od1, od2, od3, kvgrad, probs_all, ds_all
 ):
-    kvgrad, probs_all, ds_all = refs[:8], refs[8], refs[9]
-    keys = jnp.concatenate([kv[start[4 + m], 0] for m in range(8)], axis=0)
-    values = jnp.concatenate([kv[start[4 + m], 1] for m in range(8)], axis=0)
+    rows = kv.shape[0] * kv.shape[2]
+    keys, values = rows_of(kv, 0), rows_of(kv, 1)
     queries, cotans = [], []
     for block, (ref, dst) in enumerate(zip((qg0, qg1, qg2, qg3), (od0, od1, od2, od3))):
         width = ref.shape[0] * ref.shape[2]
@@ -77,21 +76,11 @@
         shape = (ref.shape[0], ref.shape[2], DH)
         dst[:, 0] = out.reshape(shape)
         dst[:, 1] = qgrad.reshape(shape)
+    shape = (kv.shape[0], kv.shape[2], DH)
     kgrad = mm(ds_all[...], jnp.concatenate(queries, axis=0), ((1,), (0,))) * SCALE
+    kvgrad[:, 0] = kgrad.astype(jnp.bfloat16).reshape(shape)
     vgrad = mm(probs_all[...], jnp.concatenate(cotans, axis=0), ((1,), (0,)))
-    for m, dst in enumerate(kvgrad):
-        group = dst.shape[1]
-        dst[0] = kgrad[m * group:(m + 1) * group].astype(jnp.bfloat16)
-        dst[1] = vgrad[m * group:(m + 1) * group].astype(jnp.bfloat16)
-
-
-def unpack_kernel(start, *refs):
-    first, second = refs[8:]
-    for m, ref in enumerate(refs[:8]):
-        width = ref.shape[2]
-        columns = pl.ds(pl.multiple_of(start[4 + m] * width, DH), width)
-        first[:, columns] = ref[0]
-        second[:, columns] = ref[1]
+    kvgrad[:, 1] = vgrad.astype(jnp.bfloat16).reshape(shape)
 
 
 def video_kernel(kv0, kv1, kv2, kv3, qg, bias, kvg0, kvg1, kvg2, kvg3, oqgrad, probs_all, ds_all):
@@ -158,59 +147,38 @@
     )(start, *blocks, video)
 
 
-def audio_grad(start, blocks, video, stats):
+def audio_grad(start, blocks, video, stats, video_grads):
     rows, tokens, heads = sizes(blocks, video)
-    part = jax.ShapeDtypeStruct((2,) + video.shape[2:], jnp.bfloat16)
-    part_block = pl.BlockSpec(part.shape[:2] + (DH,), lambda h: (0, 0, h))
     block = jax.ShapeDtypeStruct(blocks[0].shape, jnp.bfloat16)
     result = pl.pallas_call(
         audio_grad_kernel,
         grid=(heads,),
         in_specs=[pl.BlockSpec(memory_space=pltpu.SMEM)]
         + [head_block(b.shape) for b in blocks]
-        + [head_block(video.shape), pl.BlockSpec((1, 2, tokens), lambda h: (h, 0, 0))],
-        out_specs=[head_block(b.shape) for b in blocks] + [part_block] * 8,
-        out_shape=[block] * 4 + [part] * 8,
+        + [head_block(video.shape), pl.BlockSpec((1, 2, tokens), lambda h: (h, 0, 0))]
+        + [pl.BlockSpec(memory_space=pl.ANY)],
+        out_specs=[head_block(b.shape) for b in blocks] + [head_block(video.shape, 1)],
+        out_shape=[block] * 4 + [jax.ShapeDtypeStruct(video_grads.shape, jnp.bfloat16)],
         scratch_shapes=[pltpu.VMEM((rows, tokens), jnp.bfloat16)] * 2,
+        input_output_aliases={7: 4},
         compiler_params=pltpu.CompilerParams(vmem_limit_bytes=VMEM),
         cost_estimate=LONG,
         name="audio_grad",
-    )(start, *blocks, video, stats)
-    return result[:4], result[4:]
-
-
-def unpack(start, parts):
-    _, rows, columns = parts[0].shape
-    out = jax.ShapeDtypeStruct((rows, columns * 8), parts[0].dtype)
-    in_vmem = pl.BlockSpec(memory_space=pltpu.VMEM)
-    return pl.pallas_call(
-        unpack_kernel,
-        in_specs=[pl.BlockSpec(memory_space=pltpu.SMEM)] + [in_vmem] * 8,
-        out_specs=[in_vmem] * 2,
-        out_shape=[out] * 2,
-        name="unpack",
-    )(start, *parts)
-
-
-def swap(parts):
-    axes = ("xl", "zl", "core")
-    masks = [(m & 1) * 4 + m // 2 for m in range(8)]
-    return [parts[0]] + [
-        lax.ppermute(parts[m], axes, [(i, i ^ masks[m]) for i in range(8)]) for m in range(1, 8)
-    ]
+    )(start, *blocks, video, stats, video_grads)
+    return result[:4], result[4]
 
 
 def video_all(blocks, video, bias):
     rows, tokens, heads = sizes(blocks, video)
-    pair = jax.ShapeDtypeStruct((video.shape[0], 2) + video.shape[2:], jnp.bfloat16)
+    grads = (video.shape[0], 4) + video.shape[2:]
     block = jax.ShapeDtypeStruct(blocks[0].shape, jnp.bfloat16)
     result = pl.pallas_call(
         video_kernel,
         grid=(heads,),
         in_specs=[head_block(b.shape) for b in blocks]
-        + [head_block(video.shape, 1), pl.BlockSpec((tokens, DH), lambda h: (0, 0))],
+        + [head_block(video.shape), pl.BlockSpec((tokens, DH), lambda h: (0, 0))],
         out_specs=[head_block(b.shape) for b in blocks] + [head_block(video.shape)],
-        out_shape=[block] * 4 + [pair],
+        out_shape=[block] * 4 + [jax.ShapeDtypeStruct(grads, jnp.bfloat16)],
         scratch_shapes=[pltpu.VMEM((tokens, rows), jnp.bfloat16)] * 2,
         compiler_params=pltpu.CompilerParams(vmem_limit_bytes=VMEM),
         cost_estimate=LONG,
@@ -233,18 +201,17 @@
     return exchange(after(jnp.transpose(stack, (2, 0, 1, 3)), *others), HEADS8)
 
 
-def video_out(pair, *others):
-    back = jnp.transpose(exchange(after(pair, *others), HEADS8), (1, 2, 0, 3))
-    back = back.reshape(2, back.shape[1], -1)
-    return back[0], back[1]
-
-
-def plane_in(arrays):
+def video_out(stack):
+    back = jnp.transpose(exchange(stack, HEADS8), (1, 2, 0, 3))
+    return back.reshape(back.shape[0], back.shape[1], -1)
+
+
+def plane_in(arrays, *others):
     stack = jnp.stack(arrays)
     half = stack.shape[-1] // 2
     halves = jnp.stack([stack[..., :half], stack[..., half:]])
     sends = jnp.broadcast_to(halves[None], (8,) + halves.shape)
-    return exchange(sends.reshape((16,) + halves.shape[1:]), PLANE)
+    return exchange(after(sends.reshape((16,) + halves.shape[1:]), *others), PLANE)
 
 
 def plane_out(x, *others):
@@ -294,39 +261,34 @@
     tokens = alignment.shape[0]
     bias = -BIAS_SLOPE * jnp.abs(frame - alignment).astype(jnp.float32)
     start = ((y + jnp.arange(4, dtype=jnp.int32)) % 4) * (tokens // 4)
-    place = lax.axis_index("zl") * 4 + lax.axis_index("core") * 2 + lax.axis_index("xl")
-    start = jnp.concatenate([start, place ^ jnp.arange(8, dtype=jnp.int32)]).astype(jnp.int32)
     turned = lax.dynamic_slice_in_dim(jnp.tile(bias, 2), start[0], tokens)
     key_bias = jnp.broadcast_to((turned * LOG2E)[:, None], (tokens, DH))
 
-    planes = plane_in([audio_query, audio_cotan, audio_key, audio_value])
-    video = video_in([video_key, video_value, video_query, video_cotan], planes)
-    audio_qg = gather_y(planes[:, :2])
-    audio_kv = gather_y(after(planes[:, 2:], audio_qg[1], audio_qg[3]))
-
-    stats = audio_stats(start, audio_qg, video)
+    planes = plane_in([audio_query, audio_cotan])
+    audio_qg = gather_y(planes)
+    video_kv = video_in([video_key, video_value], planes)
+    planes = plane_in([audio_key, audio_value], video_kv)
+    audio_kv = gather_y(after(planes, audio_qg[1], audio_qg[3]))
+    video_qg = video_in([video_query, video_cotan], planes)
+
+    stats = audio_stats(start, audio_qg, video_kv)
     stats = after(jnp.stack([stats[:, 0] + bias, stats[:, 1]]), audio_kv[1], audio_kv[3])
     seen = jnp.stack(merge_stats(jnp.stack(gather_y(stats), axis=1), 0))
     key_bias = after(key_bias, seen)
-    seen = exchange(jnp.broadcast_to(seen[None], (8,) + seen.shape), ("zh", "xh"))
+    seen = jnp.broadcast_to(seen[None], (8,) + seen.shape)
+    seen = exchange(after(seen, video_qg), ("zh", "xh"))
     level, inner = merge_stats((seen[:, 0], seen[:, 1]), 0)
     stats = jnp.stack([level - bias, inner], axis=1)
 
-    key_value_blocks, video_oq = video_all(audio_kv, video, key_bias)
-    out_query_blocks, video_kvgrad = audio_grad(start, audio_qg, video, stats)
+    key_value_blocks, video_grads = video_all(audio_kv, video_qg, key_bias)
+    out_query_blocks, video_grads = audio_grad(start, audio_qg, video_kv, stats, video_grads)
 
     parts = scatter_y(key_value_blocks)
-    video_cross_output, video_query_grad = video_out(video_oq)
-    gate = (video_query_grad,) + tuple(parts[1:])
-    video_kvgrad = lax.optimization_barrier(tuple(video_kvgrad) + gate)[:8]
-    video_kvgrad = swap(video_kvgrad)
-    video_key_grad, video_value_grad = unpack(start, video_kvgrad)
-    sums = plane_out(add(parts), video_query_grad, out_query_blocks[0])
-    audio_key_grad, audio_value_grad = sums
-    parts = scatter_y(out_query_blocks)
-    parts = lax.optimization_barrier(tuple(parts) + tuple(video_kvgrad))[:4]
-    sums = plane_out(add(parts), audio_key_grad)
-    audio_cross_output, audio_query_grad = sums
+    grads = video_out(after(video_grads, *parts[1:]))
+    video_cross_output, video_query_grad, video_key_grad, video_value_grad = grads
+    sums = jnp.concatenate([add(parts), add(scatter_y(out_query_blocks))], axis=1)
+    sums = plane_out(sums, video_value_grad)
+    audio_key_grad, audio_value_grad, audio_cross_output, audio_query_grad = sums
     return (
         video_cross_output,
         audio_cross_output,

time: 183 us -> 182 us (level)
  waiting for transfers between devices: 58.4 us -> 77.9 us
  starting transfers between devices: 77.5 us -> 62.5 us
  other arithmetic: 9.22 us -> 6.32 us
  Pallas kernels: 26.1 us -> 24.1 us
    ppermute x15, waiting for transfers between devices: 16.3 us -> 36.2 us  [along_y(): return lax.ppermute(x, 'y', [(i, (i + step) % 4) for i in range(4)])]
    ppermute x7 -> x0, waiting for transfers between devices: 9.77 us -> none  [swap(): lax.ppermute(parts[m], axes, [(i, i ^ masks[m]) for i in range(8)])]
    ppermute x7 -> x0, starting transfers between devices: 9.75 us -> none  [swap(): lax.ppermute(parts[m], axes, [(i, i ^ masks[m]) for i in range(8)])]
    all_to_all x6 -> x7, waiting for transfers between devices: 32.3 us -> 41.7 us  [exchange(): return lax.all_to_all(x, axes, split_axis=0, concat_axis=0)]
    all_to_all x6 -> x7, starting transfers between devices: 46.4 us -> 42.1 us  [exchange(): return lax.all_to_all(x, axes, split_axis=0, concat_axis=0)]
    convert_element_type x2, other arithmetic: 2.9 us -> 0.41 us  [add(): sum((part.astype(jnp.float32) for part in parts)).astype(jnp.bfloat16)]
    pallas_call x1 -> x0, Pallas kernels: 2.17 us -> none  [unpack(): pl.pallas_call(unpack_kernel, in_specs=[pl.BlockSpec(memory_space=pltpu.S...]
    unnamed x62 -> x52, local copies, waits for them, and re-layouts: 5.33 us -> 5.37 us
  transfers between devices with their start and end apart: 28 -> 22, of which waited for: 9 -> 12; matrix products, arithmetic and copies ran while one was open for 6% -> 6% of each run, Pallas kernels for 14% -> 13%
where the time goes in v2:
time: 182 us; the launch traced here: 181 us
  waiting for transfers between devices  77.9 us (43%)
  starting transfers between devices  62.5 us (34%)
  Pallas kernels  24.1 us (13%)
  local copies, waits for them, and re-layouts  9.22 us (5%)
  other arithmetic  6.32 us (3%)
    all_to_all x7, starting transfers between devices, exchange(): return lax.all_to_all(x, axes, split_axis=0, concat_axis=0)  42.1 us
    all_to_all x7, waiting for transfers between devices, exchange(): return lax.all_to_all(x, axes, split_axis=0, concat_axis=0)  41.7 us
    ppermute x15, waiting for transfers between devices, along_y(): return lax.ppermute(x, 'y', [(i, (i + step) % 4) for i in range(4)])  36.2 us
    ppermute x15, starting transfers between devices, along_y(): return lax.ppermute(x, 'y', [(i, (i + step) % 4) for i in range(4)])  20.5 us
    pallas_call x1, Pallas kernels, video_all(): pl.pallas_call(video_kernel, grid=(heads,), in_specs=[head_block(b.shape)...  10.6 us
    pallas_call x1, Pallas kernels, audio_grad(): pl.pallas_call(audio_grad_kernel, grid=(heads,), in_specs=[pl.BlockSpec(m...  8.28 us
    unnamed x52, local copies, waits for them, and re-layouts  5.37 us
    pallas_call x1, Pallas kernels, audio_stats(): pl.pallas_call(audio_stats_kernel, grid=(heads,), in_specs=[pl.BlockSpec(...  5.14 us
  transfers between devices with their start and end apart: 22, of which 12 were waited for; matrix products, arithmetic and copies ran while one was open for 6% of the time, Pallas kernels for 13%

profile of v2, /device:TPU:33, one launch (start us, length us, event | category | flops | bytes accessed | tf_op | source)
XLA Modules:
  0.0 181.2 jit_solution(7453724153471994702)
XLA Ops:
  0.7 0.8 fusion.11
  1.5 0.8 broadcast_in_dim.8
  2.3 9.9 %all-to-all-start = ((bf16[16,2,16,384]{3,2,1,0:T(8,128)(2,1)}), bf16[16,2,16,384]{3,2,1,0:T(8,128)(2,1)S(1)}, u32[]{:S(2)}, u32[]{:S(2)}) async-start(bf16[16,2,16,384]{3,2,1,0:T(8,128)(2,1)} %bitcast.4), calls=%async_computation | async-start | bytes 786432 | tf_op jit(solution)/shard_map/all_to_all | solution.py:191
  12.4 1.0 maximum_bitcast_fusion
  13.4 11.6 %all-to-all-done.qg0 = bf16[16,2,16,384]{3,2,1,0:T(8,128)(2,1)S(1)} async-done(((bf16[16,2,16,384]{3,2,1,0:T(8,128)(2,1)}), bf16[16,2,16,384]{3,2,1,0:T(8,128)(2,1)S(1)}, u32[]{:S(2)}, u32[]{:S(2)}) %all-to-all-start) | async-done | bytes 393248 | tf_op jit(solution)/shard_map/all_to_all | solution.py:191
  25.0 6.9 %all-to-all-start.1 = ((bf16[8,2,64,384]{3,2,1,0:T(8,128)(2,1)}), bf16[8,2,64,384]{3,2,1,0:T(8,128)(2,1)S(1)}, u32[]{:S(2)}, u32[]{:S(2)}) async-start(bf16[8,2,64,384]{3,2,1,0:T(8,128)(2,1)} %maximum_bitcast_fusion), calls=%async_computation.1 | async-start | bytes 1572864 | tf_op jit(solution)/shard_map/all_to_all | solution.py:191
  31.9 1.4 collective-permute-start.2
  33.3 2.6 %collective-permute-start.1 = (bf16[16,2,16,384]{3,2,1,0:T(8,128)(2,1)S(1)}, bf16[16,2,16,384]{3,2,1,0:T(8,128)(2,1)S(1)}, u32[]{:S(2)}, u32[]{:S(2)}) collective-permute-start(bf16[16,2,16,384]{3,2,1,0:T(8,128)(2,1)S(1)} %all-to-all-done.qg0), channel_id=1, source_target_pairs={{0,128},{64,192},{128,0},{192,64},{1,129},{65,193},{129,1},{193,65... | collective-permute-start | bytes 1179656 | tf_op jit(solution)/shard_map/ppermute | solution.py:224
  35.9 1.1 collective-permute-start
  37.9 1.0 maximum_bitcast_fusion.1
  38.8 4.1 %all-to-all-done.1.kv = bf16[8,2,64,384]{3,2,1,0:T(8,128)(2,1)S(1)} async-done(((bf16[8,2,64,384]{3,2,1,0:T(8,128)(2,1)}), bf16[8,2,64,384]{3,2,1,0:T(8,128)(2,1)S(1)}, u32[]{:S(2)}, u32[]{:S(2)}) %all-to-all-start.1) | async-done | bytes 786464 | tf_op jit(solution)/shard_map/all_to_all | solution.py:191
  42.9 0.8 broadcast_in_dim.9
  43.8 4.0 %all-to-all-start.2 = ((bf16[16,2,16,384]{3,2,1,0:T(8,128)(2,1)}), bf16[16,2,16,384]{3,2,1,0:T(8,128)(2,1)S(1)}, u32[]{:S(2)}, u32[]{:S(2)}) async-start(bf16[16,2,16,384]{3,2,1,0:T(8,128)(2,1)} %bitcast.12), calls=%async_computation.2 | async-start | bytes 786432 | tf_op jit(solution)/shard_map/all_to_all | solution.py:191
  47.8 5.4 %collective-permute-done.1.qg2 = bf16[16,2,16,384]{3,2,1,0:T(8,128)(2,1)S(1)} collective-permute-done((bf16[16,2,16,384]{3,2,1,0:T(8,128)(2,1)S(1)}, bf16[16,2,16,384]{3,2,1,0:T(8,128)(2,1)S(1)}, u32[]{:S(2)}, u32[]{:S(2)}) %collective-permute-start.1) | collective-permute-done | bytes 393248 | tf_op jit(solution)/shard_map/ppermute | solution.py:224
  53.9 5.1 %audio_stats.1 = f32[3,2,1024]{2,1,0:T(2,128)} custom-call(s32[4]{0:T(128)} %copy-done.14, bf16[16,2,16,384]{3,2,1,0:T(8,128)(2,1)} %copy-done.6, bf16[16,2,16,384]{3,2,1,0:T(8,128)(2,1)} %collective-permute-done.qg1, bf16[16,2,16,384]{3,2,1,0:T(8,128)(2,1)} %copy-done.16, bf16[16,2,16,384]{3,2,1,0:T(8,128)(2,1)} %copy-done.15, bf16[8,2,64,384]{3,2,1,0:T(8,128)(2,1)} %copy-done), custom_call_target="tpu_custom_call" | custom-call | flops 49999998976 | tf_op jit(solution)/shard_map/audio_stats/pallas_call | solution.py:136
  59.1 4.1 %all-to-all-done.2.kv0 = bf16[16,2,16,384]{3,2,1,0:T(8,128)(2,1)S(1)} async-done(((bf16[16,2,16,384]{3,2,1,0:T(8,128)(2,1)}), bf16[16,2,16,384]{3,2,1,0:T(8,128)(2,1)S(1)}, u32[]{:S(2)}, u32[]{:S(2)}) %all-to-all-start.2) | async-done | bytes 393248 | tf_op jit(solution)/shard_map/all_to_all | solution.py:191
  63.2 1.3 collective-permute-start.4
  64.5 1.4 collective-permute-start.3
  65.9 4.2 %all-to-all-start.3 = ((bf16[8,2,64,384]{3,2,1,0:T(8,128)(2,1)}), bf16[8,2,64,384]{3,2,1,0:T(8,128)(2,1)S(1)}, u32[]{:S(2)}, u32[]{:S(2)}) async-start(bf16[8,2,64,384]{3,2,1,0:T(8,128)(2,1)} %maximum_bitcast_fusion.1), calls=%async_computation.3 | async-start | bytes 1572864 | tf_op jit(solution)/shard_map/all_to_all | solution.py:191
  70.2 4.2 %collective-permute-done.4.kv3 = bf16[16,2,16,384]{3,2,1,0:T(8,128)(2,1)S(1)} collective-permute-done((bf16[16,2,16,384]{3,2,1,0:T(8,128)(2,1)S(1)}, bf16[16,2,16,384]{3,2,1,0:T(8,128)(2,1)S(1)}, u32[]{:S(2)}, u32[]{:S(2)}) %collective-permute-start.4) | collective-permute-done | bytes 393248 | tf_op jit(solution)/shard_map/ppermute | solution.py:224
  74.4 0.9 collective-permute-start.7
  75.3 2.6 %collective-permute-start.6 = (f32[2,3,1024]{2,0,1:T(2,128)S(1)}, f32[2,3,1024]{2,0,1:T(2,128)S(1)}, u32[]{:S(2)}, u32[]{:S(2)}) collective-permute-start(f32[2,3,1024]{2,0,1:T(2,128)S(1)} %pad_maximum_fusion.8), channel_id=1, source_target_pairs={{0,128},{64,192},{128,0},{192,64},{1,129},{65,193},{129,1},{193,65... | collective-permute-start | bytes 73736 | tf_op jit(solution)/shard_map/ppermute | solution.py:224
  77.9 0.8 collective-permute-start.5
  78.8 0.8 collective-permute-start.8
  79.6 1.3 collective-permute-done.5
  81.3 1.0 broadcast_in_dim.11.bias
  82.2 0.8 broadcast_in_dim.10
  83.1 3.6 %all-to-all-start.4 = ((f32[8,2,3,1024]{3,1,2,0:T(2,128)}), f32[8,2,3,1024]{3,1,2,0:T(2,128)S(1)}, u32[]{:S(2)}, u32[]{:S(2)}) async-start(f32[8,2,3,1024]{3,1,2,0:T(2,128)} %broadcast_in_dim.10), calls=%async_computation.4 | async-start | bytes 393216 | tf_op jit(solution)/shard_map/all_to_all | solution.py:191
  86.6 1.5 collective-permute-done.8.kv2
  88.9 10.6 %video_all.1 = (bf16[16,2,16,384]{3,2,1,0:T(8,128)(2,1)}, bf16[16,2,16,384]{3,2,1,0:T(8,128)(2,1)}, bf16[16,2,16,384]{3,2,1,0:T(8,128)(2,1)}, bf16[16,2,16,384]{3,2,1,0:T(8,128)(2,1)}, bf16[8,4,64,384]{3,2,1,0:T(8,128)(2,1)}) custom-call(bf16[16,2,16,384]{3,2,1,0:T(8,128)(2,1)} %copy-done.7, bf16[16,2,16,384]{3,2,1,0:T(8,128)(2,1)} %copy-done.18, ...), custom_call_target="tpu_custom_call" | custom-call | flops 49999998976 | tf_op jit(solution)/shard_map/video_all/pallas_call | solution.py:175
  99.6 0.9 collective-permute-start.9
  100.4 1.7 collective-permute-start.10
  102.2 1.2 collective-permute-start.11
  104.3 8.3 %audio_grad.1 = (bf16[16,2,16,384]{3,2,1,0:T(8,128)(2,1)}, bf16[16,2,16,384]{3,2,1,0:T(8,128)(2,1)}, bf16[16,2,16,384]{3,2,1,0:T(8,128)(2,1)}, bf16[16,2,16,384]{3,2,1,0:T(8,128)(2,1)}, bf16[8,4,64,384]{3,2,1,0:T(8,128)(2,1)}) custom-call(s32[4]{0:T(128)} %copy-done.14, bf16[16,2,16,384]{3,2,1,0:T(8,128)(2,1)} %copy-done.6, ...), custom_call_target="tpu_custom_call", output_to_operand_aliasing={{4}: (7, {})} | custom-call | flops 49999998976 | tf_op jit(solution)/shard_map/audio_grad/pallas_call | solution.py:153
  112.6 4.2 %collective-permute-done.10 = bf16[16,2,16,384]{3,2,1,0:T(8,128)(2,1)S(1)} collective-permute-done((bf16[16,2,16,384]{3,2,1,0:T(8,128)(2,1)}, bf16[16,2,16,384]{3,2,1,0:T(8,128)(2,1)S(1)}, u32[]{:S(2)}, u32[]{:S(2)}) %collective-permute-start.10) | collective-permute-done | bytes 393248 | tf_op jit(solution)/shard_map/ppermute | solution.py:224
  116.8 2.8 %collective-permute-done.11 = bf16[16,2,16,384]{3,2,1,0:T(8,128)(2,1)S(1)} collective-permute-done((bf16[16,2,16,384]{3,2,1,0:T(8,128)(2,1)}, bf16[16,2,16,384]{3,2,1,0:T(8,128)(2,1)S(1)}, u32[]{:S(2)}, u32[]{:S(2)}) %collective-permute-start.11) | collective-permute-done | bytes 393248 | tf_op jit(solution)/shard_map/ppermute | solution.py:224
  119.7 5.0 %all-to-all-start.5 = ((bf16[8,4,64,384]{3,2,1,0:T(8,128)(2,1)}), bf16[8,4,64,384]{3,2,1,0:T(8,128)(2,1)S(1)}, u32[]{:S(2)}, u32[]{:S(2)}) async-start(bf16[8,4,64,384]{3,2,1,0:T(8,128)(2,1)} %get-tuple-element.39), calls=%async_computation.5 | async-start | bytes 3145728 | tf_op jit(solution)/shard_map/all_to_all | solution.py:191
  124.6 1.1 collective-permute-start.12
  125.7 2.5 %collective-permute-start.13 = (bf16[16,2,16,384]{3,2,1,0:T(8,128)(2,1)}, bf16[16,2,16,384]{3,2,1,0:T(8,128)(2,1)S(1)}, u32[]{:S(2)}, u32[]{:S(2)}) collective-permute-start(bf16[16,2,16,384]{3,2,1,0:T(8,128)(2,1)} %get-tuple-element.43), channel_id=1, source_target_pairs={{0,128},{64,192},{128,0},{192,64},{1,129},{65,193},{129,1},{193,65... | collective-permute-start | bytes 1179656 | tf_op jit(solution)/shard_map/ppermute | solution.py:224
  128.6 7.4 %collective-permute-done.12 = bf16[16,2,16,384]{3,2,1,0:T(8,128)(2,1)S(1)} collective-permute-done((bf16[16,2,16,384]{3,2,1,0:T(8,128)(2,1)}, bf16[16,2,16,384]{3,2,1,0:T(8,128)(2,1)S(1)}, u32[]{:S(2)}, u32[]{:S(2)}) %collective-permute-start.12) | collective-permute-done | bytes 393248 | tf_op jit(solution)/shard_map/ppermute | solution.py:224
  136.0 9.3 %collective-permute-done.13 = bf16[16,2,16,384]{3,2,1,0:T(8,128)(2,1)S(1)} collective-permute-done((bf16[16,2,16,384]{3,2,1,0:T(8,128)(2,1)}, bf16[16,2,16,384]{3,2,1,0:T(8,128)(2,1)S(1)}, u32[]{:S(2)}, u32[]{:S(2)}) %collective-permute-start.13) | collective-permute-done | bytes 393248 | tf_op jit(solution)/shard_map/ppermute | solution.py:224
  145.5 1.0 pad_maximum_fusion
  146.7 0.8 copy.81
  147.5 8.6 %all-to-all-start.6 = ((bf16[16,4,16,384]{3,2,1,0:T(8,128)(2,1)}), bf16[16,4,16,384]{3,2,1,0:T(8,128)(2,1)S(1)}, u32[]{:S(2)}, u32[]{:S(2)}) async-start(bf16[16,4,16,384]{3,2,1,0:T(8,128)(2,1)} %pad_maximum_fusion), calls=%async_computation.6 | async-start | bytes 1572864 | tf_op jit(solution)/shard_map/all_to_all | solution.py:191
  156.1 0.8 copy.83
  156.9 0.8 copy.82
  157.6 0.8 copy.80
  158.4 22.0 %all-to-all-done.6 = bf16[16,4,16,384]{3,2,1,0:T(8,128)(2,1)S(1)} async-done(((bf16[16,4,16,384]{3,2,1,0:T(8,128)(2,1)}), bf16[16,4,16,384]{3,2,1,0:T(8,128)(2,1)S(1)}, u32[]{:S(2)}, u32[]{:S(2)}) %all-to-all-start.6) | async-done | bytes 786464 | tf_op jit(solution)/shard_map/all_to_all | solution.py:191
  (91 shorter events, 5.4 us)
Async XLA Ops:
  0.6 11.5 %copy-start.2 = (bf16[64,3072]{1,0:T(8,128)(2,1)S(1)}, bf16[64,3072]{1,0:T(8,128)(2,1)}, u32[]{:S(2)}) copy-start(bf16[64,3072]{1,0:T(8,128)(2,1)} %param.10) | copy-start | bytes 1179652
  0.6 11.6 %copy-start.3 = (bf16[64,3072]{1,0:T(8,128)(2,1)S(1)}, bf16[64,3072]{1,0:T(8,128)(2,1)}, u32[]{:S(2)}) copy-start(bf16[64,3072]{1,0:T(8,128)(2,1)} %param.11) | copy-start | bytes 1179652
  2.3 22.7 %all-to-all-start = ((bf16[16,2,16,384]{3,2,1,0:T(8,128)(2,1)}), bf16[16,2,16,384]{3,2,1,0:T(8,128)(2,1)S(1)}, u32[]{:S(2)}, u32[]{:S(2)}) async-start(bf16[16,2,16,384]{3,2,1,0:T(8,128)(2,1)} %bitcast.4), calls=%async_computation | async-start | bytes 786432 | tf_op jit(solution)/shard_map/all_to_all | solution.py:191
  12.4 19.5 %copy-start.13 = (s32[1024]{0:T(1024)S(1)}, s32[1024]{0:T(1024)}, u32[]{:S(2)}) copy-start(s32[1024]{0:T(1024)} %param.17) | copy-start | bytes 12292
  12.4 24.7 %copy-start.4 = (bf16[64,3072]{1,0:T(8,128)(2,1)S(1)}, bf16[64,3072]{1,0:T(8,128)(2,1)}, u32[]{:S(2)}) copy-start(bf16[64,3072]{1,0:T(8,128)(2,1)} %param.9) | copy-start | bytes 1179652
  13.4 23.8 %copy-start.5 = (bf16[64,3072]{1,0:T(8,128)(2,1)S(1)}, bf16[64,3072]{1,0:T(8,128)(2,1)}, u32[]{:S(2)}) copy-start(bf16[64,3072]{1,0:T(8,128)(2,1)} %param.12) | copy-start | bytes 1179652
  25.0 12.2 %copy-start.6 = (bf16[16,2,16,384]{3,2,1,0:T(8,128)(2,1)}, bf16[16,2,16,384]{3,2,1,0:T(8,128)(2,1)S(1)}, u32[]{:S(2)}) copy-start(bf16[16,2,16,384]{3,2,1,0:T(8,128)(2,1)S(1)} %all-to-all-done.qg0) | copy-start | bytes 1179652
  25.0 17.9 %all-to-all-start.1 = ((bf16[8,2,64,384]{3,2,1,0:T(8,128)(2,1)}), bf16[8,2,64,384]{3,2,1,0:T(8,128)(2,1)S(1)}, u32[]{:S(2)}, u32[]{:S(2)}) async-start(bf16[8,2,64,384]{3,2,1,0:T(8,128)(2,1)} %maximum_bitcast_fusion), calls=%async_computation.1 | async-start | bytes 1572864 | tf_op jit(solution)/shard_map/all_to_all | solution.py:191
  31.9 15.9 %collective-permute-start.2 = (bf16[16,2,16,384]{3,2,1,0:T(8,128)(2,1)S(1)}, bf16[16,2,16,384]{3,2,1,0:T(8,128)(2,1)S(1)}, u32[]{:S(2)}, u32[]{:S(2)}) collective-permute-start(bf16[16,2,16,384]{3,2,1,0:T(8,128)(2,1)S(1)} %all-to-all-done.qg0), channel_id=1, source_target_pairs={{0,64},{64,128},{128,192},{192,0},{1,65},{65,129},{129,193},{193,1... | collective-permute-start | bytes 1179656 | tf_op jit(solution)/shard_map/ppermute | solution.py:224
  33.3 19.9 %collective-permute-start.1 = (bf16[16,2,16,384]{3,2,1,0:T(8,128)(2,1)S(1)}, bf16[16,2,16,384]{3,2,1,0:T(8,128)(2,1)S(1)}, u32[]{:S(2)}, u32[]{:S(2)}) collective-permute-start(bf16[16,2,16,384]{3,2,1,0:T(8,128)(2,1)S(1)} %all-to-all-done.qg0), channel_id=1, source_target_pairs={{0,128},{64,192},{128,0},{192,64},{1,129},{65,193},{129,1},{193,65... | collective-permute-start | bytes 1179656 | tf_op jit(solution)/shard_map/ppermute | solution.py:224
  35.9 17.3 %collective-permute-start = (bf16[16,2,16,384]{3,2,1,0:T(8,128)(2,1)S(1)}, bf16[16,2,16,384]{3,2,1,0:T(8,128)(2,1)}, u32[]{:S(2)}, u32[]{:S(2)}) collective-permute-start(bf16[16,2,16,384]{3,2,1,0:T(8,128)(2,1)S(1)} %all-to-all-done.qg0), channel_id=1, source_target_pairs={{0,192},{64,0},{128,64},{192,128},{1,193},{65,1},{129,65},{193,129... | collective-permute-start | bytes 1179656 | tf_op jit(solution)/shard_map/ppermute | solution.py:224
  37.0 0.6 copy-start.14
  37.1 0.7 copy-start.11
  37.1 0.7 copy-start.12
  42.9 10.3 %copy-start = (bf16[8,2,64,384]{3,2,1,0:T(8,128)(2,1)}, bf16[8,2,64,384]{3,2,1,0:T(8,128)(2,1)S(1)}, u32[]{:S(2)}) copy-start(bf16[8,2,64,384]{3,2,1,0:T(8,128)(2,1)S(1)} %all-to-all-done.1.kv) | copy-start | bytes 2359300
  43.8 19.4 %all-to-all-start.2 = ((bf16[16,2,16,384]{3,2,1,0:T(8,128)(2,1)}), bf16[16,2,16,384]{3,2,1,0:T(8,128)(2,1)S(1)}, u32[]{:S(2)}, u32[]{:S(2)}) async-start(bf16[16,2,16,384]{3,2,1,0:T(8,128)(2,1)} %bitcast.12), calls=%async_computation.2 | async-start | bytes 786432 | tf_op jit(solution)/shard_map/all_to_all | solution.py:191
  47.8 5.4 %copy-start.15 = (bf16[16,2,16,384]{3,2,1,0:T(8,128)(2,1)}, bf16[16,2,16,384]{3,2,1,0:T(8,128)(2,1)S(1)}, u32[]{:S(2)}) copy-start(bf16[16,2,16,384]{3,2,1,0:T(8,128)(2,1)S(1)} %collective-permute-done.2.qg3) | copy-start | bytes 1179652
  53.2 0.7 copy-start.16
  59.1 11.0 %copy-start.10 = (f32[3,2,1024]{2,1,0:T(2,128)S(1)}, f32[3,2,1024]{2,1,0:T(2,128)}, u32[]{:S(2)}) copy-start(f32[3,2,1024]{2,1,0:T(2,128)} %audio_stats.1) | copy-start | bytes 73732
  63.2 19.9 %copy-start.7 = (bf16[16,2,16,384]{3,2,1,0:T(8,128)(2,1)}, bf16[16,2,16,384]{3,2,1,0:T(8,128)(2,1)S(1)}, u32[]{:S(2)}) copy-start(bf16[16,2,16,384]{3,2,1,0:T(8,128)(2,1)S(1)} %all-to-all-done.2.kv0) | copy-start | bytes 1179652
  63.2 11.2 %collective-permute-start.4 = (bf16[16,2,16,384]{3,2,1,0:T(8,128)(2,1)S(1)}, bf16[16,2,16,384]{3,2,1,0:T(8,128)(2,1)S(1)}, u32[]{:S(2)}, u32[]{:S(2)}) collective-permute-start(bf16[16,2,16,384]{3,2,1,0:T(8,128)(2,1)S(1)} %all-to-all-done.2.kv0), channel_id=1, source_target_pairs={{0,64},{64,128},{128,192},{192,0},{1,65},{65,129},{129,193},{193,1... | collective-permute-start | bytes 1179656 | tf_op jit(solution)/shard_map/ppermute | solution.py:224
  64.5 9.9 %collective-permute-start.3 = (bf16[16,2,16,384]{3,2,1,0:T(8,128)(2,1)S(1)}, bf16[16,2,16,384]{3,2,1,0:T(8,128)(2,1)S(1)}, u32[]{:S(2)}, u32[]{:S(2)}) collective-permute-start(bf16[16,2,16,384]{3,2,1,0:T(8,128)(2,1)S(1)} %all-to-all-done.2.kv0), channel_id=1, source_target_pairs={{0,192},{64,0},{128,64},{192,128},{1,193},{65,1},{129,65},{193,129... | collective-permute-start | bytes 1179656 | tf_op jit(solution)/shard_map/ppermute | solution.py:224
  65.9 16.3 %all-to-all-start.3 = ((bf16[8,2,64,384]{3,2,1,0:T(8,128)(2,1)}), bf16[8,2,64,384]{3,2,1,0:T(8,128)(2,1)S(1)}, u32[]{:S(2)}, u32[]{:S(2)}) async-start(bf16[8,2,64,384]{3,2,1,0:T(8,128)(2,1)} %maximum_bitcast_fusion.1), calls=%async_computation.3 | async-start | bytes 1572864 | tf_op jit(solution)/shard_map/all_to_all | solution.py:191
  74.4 13.8 %copy-start.17 = (bf16[16,2,16,384]{3,2,1,0:T(8,128)(2,1)}, bf16[16,2,16,384]{3,2,1,0:T(8,128)(2,1)S(1)}, u32[]{:S(2)}) copy-start(bf16[16,2,16,384]{3,2,1,0:T(8,128)(2,1)S(1)} %collective-permute-done.4.kv3) | copy-start | bytes 1179652
  74.4 13.7 %copy-start.18 = (bf16[16,2,16,384]{3,2,1,0:T(8,128)(2,1)}, bf16[16,2,16,384]{3,2,1,0:T(8,128)(2,1)S(1)}, u32[]{:S(2)}) copy-start(bf16[16,2,16,384]{3,2,1,0:T(8,128)(2,1)S(1)} %collective-permute-done.3.kv1) | copy-start | bytes 1179652
  74.4 5.2 %collective-permute-start.7 = (f32[2,3,1024]{2,0,1:T(2,128)S(1)}, f32[2,3,1024]{2,0,1:T(2,128)S(1)}, u32[]{:S(2)}, u32[]{:S(2)}) collective-permute-start(f32[2,3,1024]{2,0,1:T(2,128)S(1)} %pad_maximum_fusion.8), channel_id=1, source_target_pairs={{0,64},{64,128},{128,192},{192,0},{1,65},{65,129},{129,193},{193,1... | collective-permute-start | bytes 73736 | tf_op jit(solution)/shard_map/ppermute | solution.py:224
  75.3 4.3 %collective-permute-start.6 = (f32[2,3,1024]{2,0,1:T(2,128)S(1)}, f32[2,3,1024]{2,0,1:T(2,128)S(1)}, u32[]{:S(2)}, u32[]{:S(2)}) collective-permute-start(f32[2,3,1024]{2,0,1:T(2,128)S(1)} %pad_maximum_fusion.8), channel_id=1, source_target_pairs={{0,128},{64,192},{128,0},{192,64},{1,129},{65,193},{129,1},{193,65... | collective-permute-start | bytes 73736 | tf_op jit(solution)/shard_map/ppermute | solution.py:224
  77.9 3.0 %collective-permute-start.5 = (f32[2,3,1024]{2,0,1:T(2,128)S(1)}, f32[2,3,1024]{2,0,1:T(2,128)S(1)}, u32[]{:S(2)}, u32[]{:S(2)}) collective-permute-start(f32[2,3,1024]{2,0,1:T(2,128)S(1)} %pad_maximum_fusion.8), channel_id=1, source_target_pairs={{0,192},{64,0},{128,64},{192,128},{1,193},{65,1},{129,65},{193,129... | collective-permute-start | bytes 73736 | tf_op jit(solution)/shard_map/ppermute | solution.py:224
  78.8 9.3 %collective-permute-start.8 = (bf16[16,2,16,384]{3,2,1,0:T(8,128)(2,1)S(1)}, bf16[16,2,16,384]{3,2,1,0:T(8,128)(2,1)S(1)}, u32[]{:S(2)}, u32[]{:S(2)}) collective-permute-start(bf16[16,2,16,384]{3,2,1,0:T(8,128)(2,1)S(1)} %all-to-all-done.2.kv0), channel_id=1, source_target_pairs={{0,128},{64,192},{128,0},{192,64},{1,129},{65,193},{129,1},{193,65... | collective-permute-start | bytes 1179656 | tf_op jit(solution)/shard_map/ppermute | solution.py:224
  82.2 5.9 %copy-start.1 = (bf16[8,2,64,384]{3,2,1,0:T(8,128)(2,1)}, bf16[8,2,64,384]{3,2,1,0:T(8,128)(2,1)S(1)}, u32[]{:S(2)}) copy-start(bf16[8,2,64,384]{3,2,1,0:T(8,128)(2,1)S(1)} %all-to-all-done.3.qg) | copy-start | bytes 2359300
  83.1 20.3 %all-to-all-start.4 = ((f32[8,2,3,1024]{3,1,2,0:T(2,128)}), f32[8,2,3,1024]{3,1,2,0:T(2,128)S(1)}, u32[]{:S(2)}, u32[]{:S(2)}) async-start(f32[8,2,3,1024]{3,1,2,0:T(2,128)} %broadcast_in_dim.10), calls=%async_computation.4 | async-start | bytes 393216 | tf_op jit(solution)/shard_map/all_to_all | solution.py:191
  88.2 0.8 copy-start.19
  99.6 13.1 %collective-permute-start.9 = (bf16[16,2,16,384]{3,2,1,0:T(8,128)(2,1)}, bf16[16,2,16,384]{3,2,1,0:T(8,128)(2,1)S(1)}, u32[]{:S(2)}, u32[]{:S(2)}) collective-permute-start(bf16[16,2,16,384]{3,2,1,0:T(8,128)(2,1)} %get-tuple-element.36), channel_id=1, source_target_pairs={{0,64},{64,128},{128,192},{192,0},{1,65},{65,129},{129,193},{193,1... | collective-permute-start | bytes 1179656 | tf_op jit(solution)/shard_map/ppermute | solution.py:224
  100.4 16.4 %collective-permute-start.10 = (bf16[16,2,16,384]{3,2,1,0:T(8,128)(2,1)}, bf16[16,2,16,384]{3,2,1,0:T(8,128)(2,1)S(1)}, u32[]{:S(2)}, u32[]{:S(2)}) collective-permute-start(bf16[16,2,16,384]{3,2,1,0:T(8,128)(2,1)} %get-tuple-element.37), channel_id=1, source_target_pairs={{0,128},{64,192},{128,0},{192,64},{1,129},{65,193},{129,1},{193,65... | collective-permute-start | bytes 1179656 | tf_op jit(solution)/shard_map/ppermute | solution.py:224
  102.2 17.5 %collective-permute-start.11 = (bf16[16,2,16,384]{3,2,1,0:T(8,128)(2,1)}, bf16[16,2,16,384]{3,2,1,0:T(8,128)(2,1)S(1)}, u32[]{:S(2)}, u32[]{:S(2)}) collective-permute-start(bf16[16,2,16,384]{3,2,1,0:T(8,128)(2,1)} %get-tuple-element.38), channel_id=1, source_target_pairs={{0,192},{64,0},{128,64},{192,128},{1,193},{65,1},{129,65},{193,129... | collective-permute-start | bytes 1179656 | tf_op jit(solution)/shard_map/ppermute | solution.py:224
  119.7 8.5 %copy-start.20 = (bf16[16,2,16,384]{3,2,1,0:T(8,128)(2,1)S(1)}, bf16[16,2,16,384]{3,2,1,0:T(8,128)(2,1)}, u32[]{:S(2)}) copy-start(bf16[16,2,16,384]{3,2,1,0:T(8,128)(2,1)} %get-tuple-element.44) | copy-start | bytes 1179652
  119.7 8.8 %copy-start.8 = (bf16[16,2,16,384]{3,2,1,0:T(8,128)(2,1)S(1)}, bf16[16,2,16,384]{3,2,1,0:T(8,128)(2,1)}, u32[]{:S(2)}) copy-start(bf16[16,2,16,384]{3,2,1,0:T(8,128)(2,1)} %get-tuple-element.40) | copy-start | bytes 1179652
  119.7 26.8 %all-to-all-start.5 = ((bf16[8,4,64,384]{3,2,1,0:T(8,128)(2,1)}), bf16[8,4,64,384]{3,2,1,0:T(8,128)(2,1)S(1)}, u32[]{:S(2)}, u32[]{:S(2)}) async-start(bf16[8,4,64,384]{3,2,1,0:T(8,128)(2,1)} %get-tuple-element.39), calls=%async_computation.5 | async-start | bytes 3145728 | tf_op jit(solution)/shard_map/all_to_all | solution.py:191
  124.6 20.7 %copy-start.9 = (bf16[16,2,16,384]{3,2,1,0:T(8,128)(2,1)S(1)}, bf16[16,2,16,384]{3,2,1,0:T(8,128)(2,1)}, u32[]{:S(2)}) copy-start(bf16[16,2,16,384]{3,2,1,0:T(8,128)(2,1)} %get-tuple-element.41) | copy-start | bytes 1179652
  124.6 11.4 %collective-permute-start.12 = (bf16[16,2,16,384]{3,2,1,0:T(8,128)(2,1)}, bf16[16,2,16,384]{3,2,1,0:T(8,128)(2,1)S(1)}, u32[]{:S(2)}, u32[]{:S(2)}) collective-permute-start(bf16[16,2,16,384]{3,2,1,0:T(8,128)(2,1)} %get-tuple-element.42), channel_id=1, source_target_pairs={{0,64},{64,128},{128,192},{192,0},{1,65},{65,129},{129,193},{193,1... | collective-permute-start | bytes 1179656 | tf_op jit(solution)/shard_map/ppermute | solution.py:224
  125.7 19.6 %collective-permute-start.13 = (bf16[16,2,16,384]{3,2,1,0:T(8,128)(2,1)}, bf16[16,2,16,384]{3,2,1,0:T(8,128)(2,1)S(1)}, u32[]{:S(2)}, u32[]{:S(2)}) collective-permute-start(bf16[16,2,16,384]{3,2,1,0:T(8,128)(2,1)} %get-tuple-element.43), channel_id=1, source_target_pairs={{0,128},{64,192},{128,0},{192,64},{1,129},{65,193},{129,1},{193,65... | collective-permute-start | bytes 1179656 | tf_op jit(solution)/shard_map/ppermute | solution.py:224
  128.2 17.1 %collective-permute-start.14 = (bf16[16,2,16,384]{3,2,1,0:T(8,128)(2,1)S(1)}, bf16[16,2,16,384]{3,2,1,0:T(8,128)(2,1)S(1)}, u32[]{:S(2)}, u32[]{:S(2)}) collective-permute-start(bf16[16,2,16,384]{3,2,1,0:T(8,128)(2,1)S(1)} %copy-done.20), channel_id=1, source_target_pairs={{0,192},{64,0},{128,64},{192,128},{1,193},{65,1},{129,65},{193,129... | collective-permute-start | bytes 1179656 | tf_op jit(solution)/shard_map/ppermute | solution.py:224
  147.5 32.9 %all-to-all-start.6 = ((bf16[16,4,16,384]{3,2,1,0:T(8,128)(2,1)}), bf16[16,4,16,384]{3,2,1,0:T(8,128)(2,1)S(1)}, u32[]{:S(2)}, u32[]{:S(2)}) async-start(bf16[16,4,16,384]{3,2,1,0:T(8,128)(2,1)} %pad_maximum_fusion), calls=%async_computation.6 | async-start | bytes 1572864 | tf_op jit(solution)/shard_map/all_to_all | solution.py:191
